TPU v7x, 256 devices: a whole 4x4x8 slice. The times are simulated.
256 devices in a mesh: req: 128 (over y_hi, x, z, core), head: 2 (over y_lo).
Axes of the slice: x: 4, y: 4 (y_hi: 2, y_lo: 2; y = y_hi * 2 + y_lo), z: 8, core: 2. Of those that a mesh axis runs over, the one named last changes fastest.
Arguments:
- queries: bfloat16 [128, 256, 8192], P('req', None, 'head'), may hold values from -17 to 17
- suffix_keys: bfloat16 [128, 256, 1024], P('req', None, 'head'), may hold values from -6 to 6
- suffix_values: bfloat16 [128, 256, 1024], P('req', None, 'head'), may hold values from -6 to 6
- node_keys: bfloat16 [256, 256, 1024], P(('req', 'head')), may hold values from -6 to 6
- node_values: bfloat16 [256, 256, 1024], P(('req', 'head')), may hold values from -6 to 6
- parents: int32 [256], P(('req', 'head')), may hold values from -1 to 255, as said below
- node_len: int32 [256], P(('req', 'head')), may hold values from 1 to 256
- req_leaf: int32 [128], P('req'), may hold values from 0 to 255, as said below
Outputs:
- attended: bfloat16 [128, 256, 8192], P('req', None, 'head')
Inputs may be any that keep to these rules, and one draw needn't show every extreme that they name: Following parents from any node reaches a root (-1) within 4 steps. `req_leaf`: each request's leaf lies exactly 3 parent steps below a root.
All inputs are finite; a program needn't handle non-finite values.
Results may differ from a plain program's by a relative error of at most 0.006.
Values may be sent and summed in bfloat16 or wider, within the bound.
No kernel may reach another device: no remote copies, remote signals or barrier semaphores. Data moves between devices by JAX's collectives and lax.ppermute only.
A program may use at most 64 MiB of HBM per device.

v0:
```python
import functools
import math

import jax
import jax.numpy as jnp
from jax import lax
from jax.experimental import pallas as pl
from jax.experimental.pallas import tpu as pltpu
from jax.sharding import PartitionSpec as P

HEAD_DIM = 128
DEPTH = 4
BLK = 16
LOW = -1e30


def spread_kernel(keys_ref, values_ref, out_ref):
    tok_blocks = keys_ref.shape[0] // BLK
    heads_all = keys_ref.shape[1] // HEAD_DIM
    heads = heads_all // 2
    for kv, ref in enumerate((keys_ref, values_ref)):
        for b in range(tok_blocks):
            for col in range(heads_all):
                group, j = divmod(col, heads)
                piece = (kv * heads + j) * tok_blocks + b
                out_ref[piece * 2 + group] = ref[
                    b * BLK:(b + 1) * BLK, col * HEAD_DIM:(col + 1) * HEAD_DIM
                ]


def spread(keys, values):
    tok, width = keys.shape
    pieces = 2 * (tok // BLK) * (width // HEAD_DIM)
    return pl.pallas_call(
        spread_kernel,
        out_shape=jax.ShapeDtypeStruct((pieces, BLK, HEAD_DIM), keys.dtype),
        in_specs=[pl.BlockSpec(memory_space=pltpu.VMEM)] * 2,
        out_specs=pl.BlockSpec(memory_space=pltpu.VMEM),
        compiler_params=pltpu.CompilerParams(vmem_limit_bytes=32 << 20),
    )(keys, values)


def pick_kernel(reqs_step, table_ref, pieces_ref, out_ref):
    nodes = pieces_ref.shape[0]
    base = pl.program_id(0) * reqs_step

    def one(r, carry):
        node = table_ref[2 * nodes + 2 * (base + r)]
        for i in range(DEPTH):
            out_ref[r, i * BLK:(i + 1) * BLK, :] = pieces_ref[node]
            if i < DEPTH - 1:
                node = table_ref[node]
        return carry

    lax.fori_loop(0, reqs_step, one, 0, unroll=8)


def pick(table, pieces, reqs):
    steps = 4
    reqs_step = reqs // steps
    return pl.pallas_call(
        functools.partial(pick_kernel, reqs_step),
        out_shape=jax.ShapeDtypeStruct((reqs, DEPTH * BLK, HEAD_DIM), pieces.dtype),
        grid_spec=pltpu.PrefetchScalarGridSpec(
            num_scalar_prefetch=1,
            grid=(steps,),
            in_specs=[pl.BlockSpec(pieces.shape, lambda s, t: (0, 0, 0))],
            out_specs=pl.BlockSpec((reqs_step, DEPTH * BLK, HEAD_DIM), lambda s, t: (s, 0, 0)),
        ),
        compiler_params=pltpu.CompilerParams(vmem_limit_bytes=32 << 20),
    )(table, pieces)


def attend_kernel(
    table_ref, me_ref, query_ref, sk_ref, sv_ref, pk_ref, pv_ref, out_ref,
    key_scr, val_scr, sval_scr,
):
    nodes = table_ref.shape[0] // 4
    blocks = pk_ref.shape[0]
    rows = DEPTH * BLK
    suf = sk_ref.shape[0]
    factor = math.log2(math.e) / math.sqrt(HEAD_DIM)

    node = table_ref[2 * nodes + 2 * me_ref[0]]
    spans = []
    for i in range(DEPTH):
        spans.append(table_ref[nodes + node])
        if i < DEPTH - 1:
            node = table_ref[node]
    tok = lax.broadcasted_iota(jnp.int32, (blocks, BLK, HEAD_DIM), 0) * BLK
    tok = tok + lax.broadcasted_iota(jnp.int32, (blocks, BLK, HEAD_DIM), 1)
    for i in range(DEPTH):
        here = slice(i * BLK, (i + 1) * BLK)
        seen = tok < spans[i]
        first = pk_ref[0, i * BLK:i * BLK + 1, :].astype(jnp.float32)
        keys = jnp.where(seen, pk_ref[:, here, :].astype(jnp.float32), first[None])
        values = jnp.where(seen, pv_ref[:, here, :].astype(jnp.float32), 0.0)
        key_scr[:, here, :] = keys.astype(jnp.bfloat16)
        val_scr[:, here, :HEAD_DIM] = values.astype(jnp.bfloat16)
        val_scr[:, here, HEAD_DIM:] = seen.astype(jnp.float32).astype(jnp.bfloat16)
    sval_scr[:, :HEAD_DIM] = sv_ref[...]
    sval_scr[:, HEAD_DIM:] = jnp.ones((suf, HEAD_DIM), jnp.bfloat16)

    pkeys = key_scr[...].reshape(blocks * rows, HEAD_DIM)
    pvals = val_scr[...].reshape(blocks * rows, 2 * HEAD_DIM)
    skeys = sk_ref[...]
    svals = sval_scr[...]
    causal = lax.broadcasted_iota(jnp.int32, (suf, suf), 0) >= lax.broadcasted_iota(
        jnp.int32, (suf, suf), 1
    )
    over = (((1,), (1,)), ((), ()))
    for g in range(query_ref.shape[1] // HEAD_DIM):
        cols = slice(g * HEAD_DIM, (g + 1) * HEAD_DIM)
        query = query_ref[:, cols]
        s1 = lax.dot_general(query, pkeys, over, preferred_element_type=jnp.float32)
        s2 = lax.dot_general(query, skeys, over, preferred_element_type=jnp.float32)
        s2 = jnp.where(causal, s2, LOW)
        top = jnp.maximum(
            jnp.max(s1, axis=1, keepdims=True), jnp.max(s2, axis=1, keepdims=True)
        )
        w1 = jnp.exp2((s1 - top) * factor).astype(jnp.bfloat16)
        w2 = jnp.exp2((s2 - top) * factor).astype(jnp.bfloat16)
        sums = jnp.dot(w1, pvals, preferred_element_type=jnp.float32)
        sums = sums + jnp.dot(w2, svals, preferred_element_type=jnp.float32)
        out_ref[:, cols] = (sums[:, :HEAD_DIM] / sums[:, HEAD_DIM:]).astype(out_ref.dtype)


def attend(table, me, queries, suffix_keys, suffix_values, prefix):
    suf, width = queries.shape
    heads = suffix_keys.shape[1] // HEAD_DIM
    blocks = prefix.shape[0] // (2 * heads)
    qwidth = width // heads
    rows = DEPTH * BLK
    return pl.pallas_call(
        attend_kernel,
        out_shape=jax.ShapeDtypeStruct((suf, width), jnp.bfloat16),
        grid_spec=pltpu.PrefetchScalarGridSpec(
            num_scalar_prefetch=2,
            grid=(heads,),
            in_specs=[
                pl.BlockSpec((suf, qwidth), lambda j, *_: (0, j)),
                pl.BlockSpec((suf, HEAD_DIM), lambda j, *_: (0, j)),
                pl.BlockSpec((suf, HEAD_DIM), lambda j, *_: (0, j)),
                pl.BlockSpec((blocks, rows, HEAD_DIM), lambda j, *_: (j, 0, 0)),
                pl.BlockSpec((blocks, rows, HEAD_DIM), lambda j, *_: (heads + j, 0, 0)),
            ],
            out_specs=pl.BlockSpec((suf, qwidth), lambda j, *_: (0, j)),
            scratch_shapes=[
                pltpu.VMEM((blocks, rows, HEAD_DIM), jnp.bfloat16),
                pltpu.VMEM((blocks, rows, 2 * HEAD_DIM), jnp.bfloat16),
                pltpu.VMEM((suf, 2 * HEAD_DIM), jnp.bfloat16),
            ],
        ),
        compiler_params=pltpu.CompilerParams(vmem_limit_bytes=48 << 20),
    )(table, me, queries, suffix_keys, suffix_values, prefix, prefix)


def share_ints(parents, node_len, req_leaf):
    axes = ("req", "head")
    count = lax.axis_size("req") * lax.axis_size("head")
    me = lax.axis_index("req") * lax.axis_size("head") + lax.axis_index("head")
    slots = jnp.arange(count, dtype=jnp.int32) == me
    zero = jnp.zeros((count,), jnp.int32)
    table = jnp.concatenate(
        [jnp.where(slots, x[0], 0) for x in (parents, node_len, req_leaf)] + [zero]
    )
    table = table.reshape(-1, 128)
    bit = 1
    while bit < count:
        table = table + lax.ppermute(table, axes, [(i, i ^ bit) for i in range(count)])
        bit *= 2
    return table.reshape(-1)


def per_device(
    queries, suffix_keys, suffix_values, node_keys, node_values, parents, node_len, req_leaf
):
    reqs = lax.axis_size("req")
    sent = spread(node_keys[0], node_values[0])
    pieces = lax.all_to_all(sent, ("req", "head"), split_axis=0, concat_axis=0, tiled=True)
    table = share_ints(parents, node_len, req_leaf)
    picked = pick(table, pieces, reqs)
    prefix = lax.all_to_all(picked, "req", split_axis=0, concat_axis=0, tiled=True)
    me = lax.axis_index("req").reshape(1)
    out = attend(table, me, queries[0], suffix_keys[0], suffix_values[0], prefix)
    return out[None]


def solution(mesh):
    in_specs = (
        P("req", None, "head"),
        P("req", None, "head"),
        P("req", None, "head"),
        P(("req", "head"), None, None),
        P(("req", "head"), None, None),
        P(("req", "head")),
        P(("req", "head")),
        P("req"),
    )
    out_specs = P("req", None, "head")
    return jax.shard_map(
        per_device, mesh=mesh, in_specs=in_specs, out_specs=out_specs, check_vma=False
    )
```

profile of v0, /device:TPU:1, one launch (start us, length us, event | category | flops | bytes accessed | tf_op | source)
XLA Modules:
  0.0 151.6 jit_solution(12561779650197020358)
XLA Ops:
  0.0 0.0 copy-start.1
  0.0 1.0 copy-done.1
  1.0 0.0 copy-start.2
  1.0 1.0 copy-done.2
  2.1 1.1 shard_map.82
  3.2 15.7 %all-to-all-start = ((bf16[256,16,128]{2,1,0:T(8,128)(2,1)}), bf16[256,16,128]{2,1,0:T(8,128)(2,1)S(1)}, u32[]{:S(2)}, u32[]{:S(2)}) async-start(bf16[256,16,128]{2,1,0:T(8,128)(2,1)} %shard_map.82), calls=%async_computation | async-start | bytes 2097152 | tf_op jit(solution)/shard_map/all_to_all | solution.py:180
  20.9 1.5 collective-permute-start
  22.4 1.4 collective-permute-done
  23.8 3.1 %collective-permute-start.1 = (s32[8,128]{1,0:T(8,128)S(1)}, s32[8,128]{1,0:T(8,128)S(1)}, u32[]{:S(2)}, u32[]{:S(2)}) collective-permute-start(s32[8,128]{1,0:T(8,128)S(1)} %fusion), channel_id=1, source_target_pairs={{0,2},{1,3},{2,0},{3,1},{4,6},{5,7},{6,4},{7,5},{8,10},{9,11},{10,... | collective-permute-start | bytes 12296 | tf_op jit(solution)/shard_map/ppermute | solution.py:170
  26.9 0.8 collective-permute-done.1
  27.7 0.0 collective-permute-start.2
  27.7 14.0 %collective-permute-done.2 = s32[8,128]{1,0:T(8,128)S(1)} collective-permute-done((s32[8,128]{1,0:T(8,128)S(1)}, s32[8,128]{1,0:T(8,128)S(1)}, u32[]{:S(2)}, u32[]{:S(2)}) %collective-permute-start.2) | collective-permute-done | bytes 4128 | tf_op jit(solution)/shard_map/ppermute | solution.py:170
  41.7 0.8 collective-permute-start.3
  42.5 2.9 %collective-permute-done.3 = s32[8,128]{1,0:T(8,128)S(1)} collective-permute-done((s32[8,128]{1,0:T(8,128)S(1)}, s32[8,128]{1,0:T(8,128)S(1)}, u32[]{:S(2)}, u32[]{:S(2)}) %collective-permute-start.3) | collective-permute-done | bytes 4128 | tf_op jit(solution)/shard_map/ppermute | solution.py:170
  45.4 5.7 %collective-permute-start.4 = (s32[8,128]{1,0:T(8,128)S(1)}, s32[8,128]{1,0:T(8,128)S(1)}, u32[]{:S(2)}, u32[]{:S(2)}) collective-permute-start(s32[8,128]{1,0:T(8,128)S(1)} %add.34), channel_id=1, source_target_pairs={{0,16},{1,17},{2,18},{3,19},{4,20},{5,21},{6,22},{7,23},{8,24},{9,... | collective-permute-start | bytes 12296 | tf_op jit(solution)/shard_map/ppermute | solution.py:170
  51.1 1.0 collective-permute-done.4
  52.1 0.9 collective-permute-start.5
  53.0 1.6 %collective-permute-done.5 = s32[8,128]{1,0:T(8,128)S(1)} collective-permute-done((s32[8,128]{1,0:T(8,128)S(1)}, s32[8,128]{1,0:T(8,128)S(1)}, u32[]{:S(2)}, u32[]{:S(2)}) %collective-permute-start.5) | collective-permute-done | bytes 4128 | tf_op jit(solution)/shard_map/ppermute | solution.py:170
  54.6 2.7 %collective-permute-start.6 = (s32[8,128]{1,0:T(8,128)S(1)}, s32[8,128]{1,0:T(8,128)S(1)}, u32[]{:S(2)}, u32[]{:S(2)}) collective-permute-start(s32[8,128]{1,0:T(8,128)S(1)} %add.36), channel_id=1, source_target_pairs={{0,64},{1,65},{2,66},{3,67},{4,68},{5,69},{6,70},{7,71},{8,72},{9,... | collective-permute-start | bytes 12296 | tf_op jit(solution)/shard_map/ppermute | solution.py:170
  57.3 1.3 collective-permute-done.6
  58.5 2.7 %collective-permute-start.7 = (s32[8,128]{1,0:T(8,128)S(1)}, s32[8,128]{1,0:T(8,128)S(1)}, u32[]{:S(2)}, u32[]{:S(2)}) collective-permute-start(s32[8,128]{1,0:T(8,128)S(1)} %add.37), channel_id=1, source_target_pairs={{0,128},{1,129},{2,130},{3,131},{4,132},{5,133},{6,134},{7,135},{8... | collective-permute-start | bytes 12296 | tf_op jit(solution)/shard_map/ppermute | solution.py:170
  61.3 1.2 collective-permute-done.7
  62.5 0.0 all-to-all-done.pieces_ref
  62.5 1.3 shard_map.83
  63.8 0.0 copy-start
  63.8 0.0 copy-start.3
  63.9 0.0 copy-start.4
  63.9 71.7 %all_to_all.10.pk_ref.pv_ref = bf16[128,64,128]{2,1,0:T(8,128)(2,1)S(1)} all-to-all(bf16[128,64,128]{2,1,0:T(8,128)(2,1)S(1)} %shard_map.83), channel_id=1, replica_groups=mesh['req'=128,'head'=2] {'req'}, dimensions={0} | all-to-all | bytes 4194304 | tf_op jit(solution)/shard_map/all_to_all | solution.py:183
  135.6 0.0 copy-done
  135.6 0.0 copy-done.3
  135.6 0.0 copy-done.4
  135.6 16.0 %shard_map.84 = bf16[256,4096]{1,0:T(8,128)(2,1)} custom-call(s32[1024]{0:T(1024)S(1)} %add_bitcast_fusion.table_ref, s32[1]{0:T(128)} %bitcast.4.me_ref, bf16[256,4096]{1,0:T(8,128)(2,1)S(1)} %bitcast.15, bf16[256,512]{1,0:T(8,128)(2,1)S(1)} %bitcast.18, bf16[256,512]{1,0:T(8,128)(2,1)S(1)} %bitcast.19, bf16[128,64,128]{2,1,0:T(8,128)(2,1)S(1)} %all_to_all.10.pk_ref.pv_ref, ...), custom_call_target="tpu_custom_call" | custom-call | tf_op jit(solution)/shard_map/pallas_call | solution.py:134
  (12 shorter events, 0.1 us)
Async XLA Ops:
  0.0 1.0 copy-start.1
  1.0 1.0 copy-start.2
  3.2 59.3 %all-to-all-start = ((bf16[256,16,128]{2,1,0:T(8,128)(2,1)}), bf16[256,16,128]{2,1,0:T(8,128)(2,1)S(1)}, u32[]{:S(2)}, u32[]{:S(2)}) async-start(bf16[256,16,128]{2,1,0:T(8,128)(2,1)} %shard_map.82), calls=%async_computation | async-start | bytes 2097152 | tf_op jit(solution)/shard_map/all_to_all | solution.py:180
  20.9 2.9 %collective-permute-start = (s32[8,128]{1,0:T(8,128)S(1)}, s32[8,128]{1,0:T(8,128)S(1)}, u32[]{:S(2)}, u32[]{:S(2)}) collective-permute-start(s32[8,128]{1,0:T(8,128)S(1)} %pad_add_fusion), channel_id=1, source_target_pairs={{0,1},{1,0},{2,3},{3,2},{4,5},{5,4},{6,7},{7,6},{8,9},{9,8},{10,11... | collective-permute-start | bytes 12296 | tf_op jit(solution)/shard_map/ppermute | solution.py:170
  23.8 3.9 %collective-permute-start.1 = (s32[8,128]{1,0:T(8,128)S(1)}, s32[8,128]{1,0:T(8,128)S(1)}, u32[]{:S(2)}, u32[]{:S(2)}) collective-permute-start(s32[8,128]{1,0:T(8,128)S(1)} %fusion), channel_id=1, source_target_pairs={{0,2},{1,3},{2,0},{3,1},{4,6},{5,7},{6,4},{7,5},{8,10},{9,11},{10,... | collective-permute-start | bytes 12296 | tf_op jit(solution)/shard_map/ppermute | solution.py:170
  27.7 14.0 %collective-permute-start.2 = (s32[8,128]{1,0:T(8,128)S(1)}, s32[8,128]{1,0:T(8,128)S(1)}, u32[]{:S(2)}, u32[]{:S(2)}) collective-permute-start(s32[8,128]{1,0:T(8,128)S(1)} %add.32), channel_id=1, source_target_pairs={{0,4},{1,5},{2,6},{3,7},{4,0},{5,1},{6,2},{7,3},{8,12},{9,13},{10,... | collective-permute-start | bytes 12296 | tf_op jit(solution)/shard_map/ppermute | solution.py:170
  41.7 3.7 %collective-permute-start.3 = (s32[8,128]{1,0:T(8,128)S(1)}, s32[8,128]{1,0:T(8,128)S(1)}, u32[]{:S(2)}, u32[]{:S(2)}) collective-permute-start(s32[8,128]{1,0:T(8,128)S(1)} %add.33), channel_id=1, source_target_pairs={{0,8},{1,9},{2,10},{3,11},{4,12},{5,13},{6,14},{7,15},{8,0},{9,1},... | collective-permute-start | bytes 12296 | tf_op jit(solution)/shard_map/ppermute | solution.py:170
  45.4 6.7 %collective-permute-start.4 = (s32[8,128]{1,0:T(8,128)S(1)}, s32[8,128]{1,0:T(8,128)S(1)}, u32[]{:S(2)}, u32[]{:S(2)}) collective-permute-start(s32[8,128]{1,0:T(8,128)S(1)} %add.34), channel_id=1, source_target_pairs={{0,16},{1,17},{2,18},{3,19},{4,20},{5,21},{6,22},{7,23},{8,24},{9,... | collective-permute-start | bytes 12296 | tf_op jit(solution)/shard_map/ppermute | solution.py:170
  52.1 2.5 %collective-permute-start.5 = (s32[8,128]{1,0:T(8,128)S(1)}, s32[8,128]{1,0:T(8,128)S(1)}, u32[]{:S(2)}, u32[]{:S(2)}) collective-permute-start(s32[8,128]{1,0:T(8,128)S(1)} %add.35), channel_id=1, source_target_pairs={{0,32},{1,33},{2,34},{3,35},{4,36},{5,37},{6,38},{7,39},{8,40},{9,... | collective-permute-start | bytes 12296 | tf_op jit(solution)/shard_map/ppermute | solution.py:170
  54.6 4.0 %collective-permute-start.6 = (s32[8,128]{1,0:T(8,128)S(1)}, s32[8,128]{1,0:T(8,128)S(1)}, u32[]{:S(2)}, u32[]{:S(2)}) collective-permute-start(s32[8,128]{1,0:T(8,128)S(1)} %add.36), channel_id=1, source_target_pairs={{0,64},{1,65},{2,66},{3,67},{4,68},{5,69},{6,70},{7,71},{8,72},{9,... | collective-permute-start | bytes 12296 | tf_op jit(solution)/shard_map/ppermute | solution.py:170
  58.5 4.0 %collective-permute-start.7 = (s32[8,128]{1,0:T(8,128)S(1)}, s32[8,128]{1,0:T(8,128)S(1)}, u32[]{:S(2)}, u32[]{:S(2)}) collective-permute-start(s32[8,128]{1,0:T(8,128)S(1)} %add.37), channel_id=1, source_target_pairs={{0,128},{1,129},{2,130},{3,131},{4,132},{5,133},{6,134},{7,135},{8... | collective-permute-start | bytes 12296 | tf_op jit(solution)/shard_map/ppermute | solution.py:170
  63.8 71.8 %copy-start = (bf16[1,256,4096]{2,1,0:T(8,128)(2,1)S(1)}, bf16[1,256,4096]{2,1,0:T(8,128)(2,1)}, u32[]{:S(2)}) copy-start(bf16[1,256,4096]{2,1,0:T(8,128)(2,1)} %param.8) | copy-start | bytes 6291460
  63.8 71.7 %copy-start.3 = (bf16[1,256,512]{2,1,0:T(8,128)(2,1)S(1)}, bf16[1,256,512]{2,1,0:T(8,128)(2,1)}, u32[]{:S(2)}) copy-start(bf16[1,256,512]{2,1,0:T(8,128)(2,1)} %param.9) | copy-start | bytes 786436
  63.9 71.7 %copy-start.4 = (bf16[1,256,512]{2,1,0:T(8,128)(2,1)S(1)}, bf16[1,256,512]{2,1,0:T(8,128)(2,1)}, u32[]{:S(2)}) copy-start(bf16[1,256,512]{2,1,0:T(8,128)(2,1)} %param.10) | copy-start | bytes 786436
where the time goes:
time: 152 us
  blocking collectives  71.7 us (47%)
  starting transfers between devices  33.1 us (22%)
  waiting for transfers between devices  24.1 us (16%)
  Pallas kernels  18.5 us (12%)
  local copies, waits for them, and re-layouts  2.1 us (1%)
  between operations  2.04 us (1%)
    all_to_all x1, blocking collectives, per_device(): lax.all_to_all(picked, 'req', split_axis=0, concat_axis=0, tiled=True)  71.7 us
    ppermute x8, waiting for transfers between devices, share_ints(): lax.ppermute(table, axes, [(i, i ^ bit) for i in range(count)])  24.1 us
    ppermute x8, starting transfers between devices, share_ints(): lax.ppermute(table, axes, [(i, i ^ bit) for i in range(count)])  17.4 us
    pallas_call x1, Pallas kernels, attend(): pl.pallas_call(attend_kernel, out_shape=jax.ShapeDtypeStruct((suf, width)...  16 us
    all_to_all x1, starting transfers between devices, per_device(): lax.all_to_all(sent, ('req', 'head'), split_axis=0, concat_axis=0, tiled=...  15.7 us
  transfers between devices with their start and end apart: 9, of which 8 were waited for; matrix products, arithmetic and copies ran while one was open for 0% of the time, Pallas kernels for 0%

commit v1 on v0

--- a/solution.py
+++ b/solution.py
@@ -14,30 +14,38 @@
 LOW = -1e30
 
 
-def spread_kernel(keys_ref, values_ref, out_ref):
-    tok_blocks = keys_ref.shape[0] // BLK
-    heads_all = keys_ref.shape[1] // HEAD_DIM
-    heads = heads_all // 2
+def spread_kernel(keys_ref, values_ref, out_ref, sems):
+    _, heads, _, groups, _, _ = out_ref.shape
+    copies = []
     for kv, ref in enumerate((keys_ref, values_ref)):
-        for b in range(tok_blocks):
-            for col in range(heads_all):
-                group, j = divmod(col, heads)
-                piece = (kv * heads + j) * tok_blocks + b
-                out_ref[piece * 2 + group] = ref[
-                    b * BLK:(b + 1) * BLK, col * HEAD_DIM:(col + 1) * HEAD_DIM
-                ]
-
-
-def spread(keys, values):
+        for group in range(groups):
+            for j in range(heads):
+                col = (group * heads + j) * HEAD_DIM
+                copies.append(
+                    pltpu.make_async_copy(
+                        ref.at[:, :, col:col + HEAD_DIM],
+                        out_ref.at[kv, j, :, group],
+                        sems.at[len(copies)],
+                    )
+                )
+    for copy in copies:
+        copy.start()
+    for copy in copies:
+        copy.wait()
+
+
+def spread(keys, values, groups):
     tok, width = keys.shape
-    pieces = 2 * (tok // BLK) * (width // HEAD_DIM)
-    return pl.pallas_call(
+    blocks, heads = tok // BLK, width // HEAD_DIM // groups
+    out = pl.pallas_call(
         spread_kernel,
-        out_shape=jax.ShapeDtypeStruct((pieces, BLK, HEAD_DIM), keys.dtype),
-        in_specs=[pl.BlockSpec(memory_space=pltpu.VMEM)] * 2,
-        out_specs=pl.BlockSpec(memory_space=pltpu.VMEM),
-        compiler_params=pltpu.CompilerParams(vmem_limit_bytes=32 << 20),
-    )(keys, values)
+        out_shape=jax.ShapeDtypeStruct((2, heads, blocks, groups, BLK, HEAD_DIM), keys.dtype),
+        in_specs=[pl.BlockSpec(memory_space=pl.ANY)] * 2,
+        out_specs=pl.BlockSpec(memory_space=pl.ANY),
+        scratch_shapes=[pltpu.SemaphoreType.DMA((2 * groups * heads,))],
+        compiler_params=pltpu.CompilerParams(vmem_limit_bytes=60 << 20),
+    )(keys.reshape(blocks, BLK, width), values.reshape(blocks, BLK, width))
+    return out.reshape(-1, BLK, HEAD_DIM)
 
 
 def pick_kernel(reqs_step, table_ref, pieces_ref, out_ref):
@@ -165,10 +173,14 @@
         [jnp.where(slots, x[0], 0) for x in (parents, node_len, req_leaf)] + [zero]
     )
     table = table.reshape(-1, 128)
-    bit = 1
-    while bit < count:
-        table = table + lax.ppermute(table, axes, [(i, i ^ bit) for i in range(count)])
-        bit *= 2
+    for bits in ((0, 1), (5, 6), (7,), (3, 4), (2,)):
+        flips = [0]
+        for bit in bits:
+            flips += [flip | 1 << bit for flip in flips]
+        total = table
+        for flip in flips[1:]:
+            total = total + lax.ppermute(table, axes, [(i, i ^ flip) for i in range(count)])
+        table = total
     return table.reshape(-1)
 
 
@@ -176,7 +188,7 @@
     queries, suffix_keys, suffix_values, node_keys, node_values, parents, node_len, req_leaf
 ):
     reqs = lax.axis_size("req")
-    sent = spread(node_keys[0], node_values[0])
+    sent = spread(node_keys[0], node_values[0], lax.axis_size("head"))
     pieces = lax.all_to_all(sent, ("req", "head"), split_axis=0, concat_axis=0, tiled=True)
     table = share_ints(parents, node_len, req_leaf)
     picked = pick(table, pieces, reqs)

time: 152 us -> 165 us (1.086)
  Pallas kernels: 18.5 us -> 50.3 us
  waiting for transfers between devices: 24.1 us -> 13.1 us
  blocking collectives: 71.7 us -> 66.5 us
  local copies, waits for them, and re-layouts: 2.1 us -> 0.02 us
    pallas_call x1, Pallas kernels: 1.15 us -> 33 us  [spread(): pl.pallas_call(spread_kernel, out_shape=jax.ShapeDtypeStruct((2, heads, b...]
    ppermute x8 -> x11, waiting for transfers between devices: 24.1 us -> 13.1 us  [share_ints(): lax.ppermute(table, axes, [(i, i ^ flip) for i in range(count)])]
    all_to_all x1, blocking collectives: 71.7 us -> 66.5 us  [per_device(): lax.all_to_all(picked, 'req', split_axis=0, concat_axis=0, tiled=True)]
    unnamed x10 -> x6, local copies, waits for them, and re-layouts: 2.1 us -> 0.02 us
    ppermute x8 -> x11, starting transfers between devices: 17.4 us -> 17.1 us  [share_ints(): lax.ppermute(table, axes, [(i, i ^ flip) for i in range(count)])]
  transfers between devices with their start and end apart: 9 -> 12, of which waited for: 8 -> 7; matrix products, arithmetic and copies ran while one was open for 0% -> 0% of each run, Pallas kernels for 0% -> 0%
where the time goes in v1:
time: 165 us
  blocking collectives  66.5 us (40%)
  Pallas kernels  50.3 us (30%)
  starting transfers between devices  32.7 us (20%)
  waiting for transfers between devices  13.1 us (8%)
  between operations  2.05 us (1%)
    all_to_all x1, blocking collectives, per_device(): lax.all_to_all(picked, 'req', split_axis=0, concat_axis=0, tiled=True)  66.5 us
    pallas_call x1, Pallas kernels, spread(): pl.pallas_call(spread_kernel, out_shape=jax.ShapeDtypeStruct((2, heads, b...  33 us
    ppermute x11, starting transfers between devices, share_ints(): lax.ppermute(table, axes, [(i, i ^ flip) for i in range(count)])  17.1 us
    pallas_call x1, Pallas kernels, attend(): pl.pallas_call(attend_kernel, out_shape=jax.ShapeDtypeStruct((suf, width)...  16 us
    all_to_all x1, starting transfers between devices, per_device(): lax.all_to_all(sent, ('req', 'head'), split_axis=0, concat_axis=0, tiled=...  15.7 us
    ppermute x11, waiting for transfers between devices, share_ints(): lax.ppermute(table, axes, [(i, i ^ flip) for i in range(count)])  13.1 us
  transfers between devices with their start and end apart: 12, of which 7 were waited for; matrix products, arithmetic and copies ran while one was open for 0% of the time, Pallas kernels for 0%

profile of v1, /device:TPU:1, one launch (start us, length us, event | category | flops | bytes accessed | tf_op | source)
XLA Modules:
  0.0 164.8 jit_solution(10207452983008183604)
XLA Ops:
  0.0 33.0 %shard_map.82 = bf16[2,4,16,2,16,128]{5,4,3,2,1,0:T(8,128)(2,1)} custom-call(bf16[16,16,1024]{2,1,0:T(8,128)(2,1)} %bitcast.20, bf16[16,16,1024]{2,1,0:T(8,128)(2,1)} %bitcast.21), custom_call_target="tpu_custom_call" | custom-call | tf_op jit(solution)/shard_map/pallas_call | solution.py:40
  33.0 15.7 %all-to-all-start = ((bf16[256,16,128]{2,1,0:T(8,128)(2,1)}), bf16[256,16,128]{2,1,0:T(8,128)(2,1)S(1)}, u32[]{:S(2)}, u32[]{:S(2)}) async-start(bf16[256,16,128]{2,1,0:T(8,128)(2,1)} %bitcast.19), calls=%async_computation | async-start | bytes 2097152 | tf_op jit(solution)/shard_map/all_to_all | solution.py:192
  50.7 2.2 %collective-permute-start.1 = (s32[8,128]{1,0:T(8,128)S(1)}, s32[8,128]{1,0:T(8,128)S(1)}, u32[]{:S(2)}, u32[]{:S(2)}) collective-permute-start(s32[8,128]{1,0:T(8,128)S(1)} %pad_add_fusion), channel_id=1, source_target_pairs={{0,2},{1,3},{2,0},{3,1},{4,6},{5,7},{6,4},{7,5},{8,10},{9,11},{10,... | collective-permute-start | bytes 12296 | tf_op jit(solution)/shard_map/ppermute | solution.py:182
  52.9 0.0 collective-permute-start.2
  52.9 1.4 collective-permute-start
  54.4 0.0 collective-permute-done.1
  54.4 1.9 %collective-permute-done.2 = s32[8,128]{1,0:T(8,128)S(1)} collective-permute-done((s32[8,128]{1,0:T(8,128)S(1)}, s32[8,128]{1,0:T(8,128)S(1)}, u32[]{:S(2)}, u32[]{:S(2)}) %collective-permute-start.2) | collective-permute-done | bytes 4128 | tf_op jit(solution)/shard_map/ppermute | solution.py:182
  56.3 0.0 collective-permute-done
  56.3 1.7 %collective-permute-start.5 = (s32[8,128]{1,0:T(8,128)S(1)}, s32[8,128]{1,0:T(8,128)S(1)}, u32[]{:S(2)}, u32[]{:S(2)}) collective-permute-start(s32[8,128]{1,0:T(8,128)S(1)} %add_add_fusion.2), channel_id=1, source_target_pairs={{0,96},{1,97},{2,98},{3,99},{4,100},{5,101},{6,102},{7,103},{8,104... | collective-permute-start | bytes 12296 | tf_op jit(solution)/shard_map/ppermute | solution.py:182
  58.0 0.5 collective-permute-start.4
  58.5 1.2 collective-permute-start.3
  59.6 0.7 collective-permute-done.5
  60.4 1.9 %collective-permute-done.4 = s32[8,128]{1,0:T(8,128)S(1)} collective-permute-done((s32[8,128]{1,0:T(8,128)S(1)}, s32[8,128]{1,0:T(8,128)S(1)}, u32[]{:S(2)}, u32[]{:S(2)}) %collective-permute-start.4) | collective-permute-done | bytes 4128 | tf_op jit(solution)/shard_map/ppermute | solution.py:182
  62.2 0.0 collective-permute-done.3
  62.3 2.6 %collective-permute-start.6 = (s32[8,128]{1,0:T(8,128)S(1)}, s32[8,128]{1,0:T(8,128)S(1)}, u32[]{:S(2)}, u32[]{:S(2)}) collective-permute-start(s32[8,128]{1,0:T(8,128)S(1)} %add_add_fusion.1), channel_id=1, source_target_pairs={{0,128},{1,129},{2,130},{3,131},{4,132},{5,133},{6,134},{7,135},{8... | collective-permute-start | bytes 12296 | tf_op jit(solution)/shard_map/ppermute | solution.py:182
  64.8 1.8 %collective-permute-done.6 = s32[8,128]{1,0:T(8,128)S(1)} collective-permute-done((s32[8,128]{1,0:T(8,128)S(1)}, s32[8,128]{1,0:T(8,128)S(1)}, u32[]{:S(2)}, u32[]{:S(2)}) %collective-permute-start.6) | collective-permute-done | bytes 4128 | tf_op jit(solution)/shard_map/ppermute | solution.py:182
  66.6 4.8 %collective-permute-start.9 = (s32[8,128]{1,0:T(8,128)S(1)}, s32[8,128]{1,0:T(8,128)S(1)}, u32[]{:S(2)}, u32[]{:S(2)}) collective-permute-start(s32[8,128]{1,0:T(8,128)S(1)} %add.46), channel_id=1, source_target_pairs={{0,24},{1,25},{2,26},{3,27},{4,28},{5,29},{6,30},{7,31},{8,16},{9,... | collective-permute-start | bytes 12296 | tf_op jit(solution)/shard_map/ppermute | solution.py:182
  71.4 1.3 collective-permute-start.8
  72.7 0.8 collective-permute-start.7
  73.5 0.8 collective-permute-done.9
  74.3 3.7 %collective-permute-done.8 = s32[8,128]{1,0:T(8,128)S(1)} collective-permute-done((s32[8,128]{1,0:T(8,128)S(1)}, s32[8,128]{1,0:T(8,128)S(1)}, u32[]{:S(2)}, u32[]{:S(2)}) %collective-permute-start.8) | collective-permute-done | bytes 4128 | tf_op jit(solution)/shard_map/ppermute | solution.py:182
  78.1 0.0 collective-permute-done.7
  78.1 0.6 collective-permute-start.10
  78.7 2.2 %collective-permute-done.10 = s32[8,128]{1,0:T(8,128)S(1)} collective-permute-done((s32[8,128]{1,0:T(8,128)S(1)}, s32[8,128]{1,0:T(8,128)S(1)}, u32[]{:S(2)}, u32[]{:S(2)}) %collective-permute-start.10) | collective-permute-done | bytes 4128 | tf_op jit(solution)/shard_map/ppermute | solution.py:182
  80.9 0.0 all-to-all-done.pieces_ref
  80.9 1.3 shard_map.83
  82.2 0.0 copy-start
  82.3 0.0 copy-start.1
  82.3 0.0 copy-start.2
  82.3 66.5 %all_to_all.10.pk_ref.pv_ref = bf16[128,64,128]{2,1,0:T(8,128)(2,1)S(1)} all-to-all(bf16[128,64,128]{2,1,0:T(8,128)(2,1)S(1)} %shard_map.83), channel_id=1, replica_groups=mesh['req'=128,'head'=2] {'req'}, dimensions={0} | all-to-all | bytes 4194304 | tf_op jit(solution)/shard_map/all_to_all | solution.py:195
  148.8 0.0 copy-done
  148.8 0.0 copy-done.1
  148.8 0.0 copy-done.2
  148.8 16.0 %shard_map.84 = bf16[256,4096]{1,0:T(8,128)(2,1)} custom-call(s32[1024]{0:T(1024)S(1)} %add_bitcast_fusion.table_ref, s32[1]{0:T(128)} %bitcast.4.me_ref, bf16[256,4096]{1,0:T(8,128)(2,1)S(1)} %bitcast.16, bf16[256,512]{1,0:T(8,128)(2,1)S(1)} %bitcast.17, bf16[256,512]{1,0:T(8,128)(2,1)S(1)} %bitcast.18, bf16[128,64,128]{2,1,0:T(8,128)(2,1)S(1)} %all_to_all.10.pk_ref.pv_ref, ...), custom_call_target="tpu_custom_call" | custom-call | tf_op jit(solution)/shard_map/pallas_call | solution.py:142
  (9 shorter events, 0.1 us)
Async XLA Ops:
  33.0 47.9 %all-to-all-start = ((bf16[256,16,128]{2,1,0:T(8,128)(2,1)}), bf16[256,16,128]{2,1,0:T(8,128)(2,1)S(1)}, u32[]{:S(2)}, u32[]{:S(2)}) async-start(bf16[256,16,128]{2,1,0:T(8,128)(2,1)} %bitcast.19), calls=%async_computation | async-start | bytes 2097152 | tf_op jit(solution)/shard_map/all_to_all | solution.py:192
  50.7 3.7 %collective-permute-start.1 = (s32[8,128]{1,0:T(8,128)S(1)}, s32[8,128]{1,0:T(8,128)S(1)}, u32[]{:S(2)}, u32[]{:S(2)}) collective-permute-start(s32[8,128]{1,0:T(8,128)S(1)} %pad_add_fusion), channel_id=1, source_target_pairs={{0,2},{1,3},{2,0},{3,1},{4,6},{5,7},{6,4},{7,5},{8,10},{9,11},{10,... | collective-permute-start | bytes 12296 | tf_op jit(solution)/shard_map/ppermute | solution.py:182
  52.9 3.4 %collective-permute-start.2 = (s32[8,128]{1,0:T(8,128)S(1)}, s32[8,128]{1,0:T(8,128)S(1)}, u32[]{:S(2)}, u32[]{:S(2)}) collective-permute-start(s32[8,128]{1,0:T(8,128)S(1)} %pad_add_fusion), channel_id=1, source_target_pairs={{0,3},{1,2},{2,1},{3,0},{4,7},{5,6},{6,5},{7,4},{8,11},{9,10},{10,... | collective-permute-start | bytes 12296 | tf_op jit(solution)/shard_map/ppermute | solution.py:182
  52.9 3.4 %collective-permute-start = (s32[8,128]{1,0:T(8,128)S(1)}, s32[8,128]{1,0:T(8,128)S(1)}, u32[]{:S(2)}, u32[]{:S(2)}) collective-permute-start(s32[8,128]{1,0:T(8,128)S(1)} %pad_add_fusion), channel_id=1, source_target_pairs={{0,1},{1,0},{2,3},{3,2},{4,5},{5,4},{6,7},{7,6},{8,9},{9,8},{10,11... | collective-permute-start | bytes 12296 | tf_op jit(solution)/shard_map/ppermute | solution.py:182
  56.3 4.1 %collective-permute-start.5 = (s32[8,128]{1,0:T(8,128)S(1)}, s32[8,128]{1,0:T(8,128)S(1)}, u32[]{:S(2)}, u32[]{:S(2)}) collective-permute-start(s32[8,128]{1,0:T(8,128)S(1)} %add_add_fusion.2), channel_id=1, source_target_pairs={{0,96},{1,97},{2,98},{3,99},{4,100},{5,101},{6,102},{7,103},{8,104... | collective-permute-start | bytes 12296 | tf_op jit(solution)/shard_map/ppermute | solution.py:182
  58.0 4.3 %collective-permute-start.4 = (s32[8,128]{1,0:T(8,128)S(1)}, s32[8,128]{1,0:T(8,128)S(1)}, u32[]{:S(2)}, u32[]{:S(2)}) collective-permute-start(s32[8,128]{1,0:T(8,128)S(1)} %add_add_fusion.2), channel_id=1, source_target_pairs={{0,64},{1,65},{2,66},{3,67},{4,68},{5,69},{6,70},{7,71},{8,72},{9,... | collective-permute-start | bytes 12296 | tf_op jit(solution)/shard_map/ppermute | solution.py:182
  58.5 3.8 %collective-permute-start.3 = (s32[8,128]{1,0:T(8,128)S(1)}, s32[8,128]{1,0:T(8,128)S(1)}, u32[]{:S(2)}, u32[]{:S(2)}) collective-permute-start(s32[8,128]{1,0:T(8,128)S(1)} %add_add_fusion.2), channel_id=1, source_target_pairs={{0,32},{1,33},{2,34},{3,35},{4,36},{5,37},{6,38},{7,39},{8,40},{9,... | collective-permute-start | bytes 12296 | tf_op jit(solution)/shard_map/ppermute | solution.py:182
  62.3 4.4 %collective-permute-start.6 = (s32[8,128]{1,0:T(8,128)S(1)}, s32[8,128]{1,0:T(8,128)S(1)}, u32[]{:S(2)}, u32[]{:S(2)}) collective-permute-start(s32[8,128]{1,0:T(8,128)S(1)} %add_add_fusion.1), channel_id=1, source_target_pairs={{0,128},{1,129},{2,130},{3,131},{4,132},{5,133},{6,134},{7,135},{8... | collective-permute-start | bytes 12296 | tf_op jit(solution)/shard_map/ppermute | solution.py:182
  66.6 7.7 %collective-permute-start.9 = (s32[8,128]{1,0:T(8,128)S(1)}, s32[8,128]{1,0:T(8,128)S(1)}, u32[]{:S(2)}, u32[]{:S(2)}) collective-permute-start(s32[8,128]{1,0:T(8,128)S(1)} %add.46), channel_id=1, source_target_pairs={{0,24},{1,25},{2,26},{3,27},{4,28},{5,29},{6,30},{7,31},{8,16},{9,... | collective-permute-start | bytes 12296 | tf_op jit(solution)/shard_map/ppermute | solution.py:182
  71.4 6.7 %collective-permute-start.8 = (s32[8,128]{1,0:T(8,128)S(1)}, s32[8,128]{1,0:T(8,128)S(1)}, u32[]{:S(2)}, u32[]{:S(2)}) collective-permute-start(s32[8,128]{1,0:T(8,128)S(1)} %add.46), channel_id=1, source_target_pairs={{0,16},{1,17},{2,18},{3,19},{4,20},{5,21},{6,22},{7,23},{8,24},{9,... | collective-permute-start | bytes 12296 | tf_op jit(solution)/shard_map/ppermute | solution.py:182
  72.7 5.4 %collective-permute-start.7 = (s32[8,128]{1,0:T(8,128)S(1)}, s32[8,128]{1,0:T(8,128)S(1)}, u32[]{:S(2)}, u32[]{:S(2)}) collective-permute-start(s32[8,128]{1,0:T(8,128)S(1)} %add.46), channel_id=1, source_target_pairs={{0,8},{1,9},{2,10},{3,11},{4,12},{5,13},{6,14},{7,15},{8,0},{9,1},... | collective-permute-start | bytes 12296 | tf_op jit(solution)/shard_map/ppermute | solution.py:182
  78.1 2.8 %collective-permute-start.10 = (s32[8,128]{1,0:T(8,128)S(1)}, s32[8,128]{1,0:T(8,128)S(1)}, u32[]{:S(2)}, u32[]{:S(2)}) collective-permute-start(s32[8,128]{1,0:T(8,128)S(1)} %add_add_fusion), channel_id=1, source_target_pairs={{0,4},{1,5},{2,6},{3,7},{4,0},{5,1},{6,2},{7,3},{8,12},{9,13},{10,... | collective-permute-start | bytes 12296 | tf_op jit(solution)/shard_map/ppermute | solution.py:182
  82.2 66.6 %copy-start = (bf16[1,256,4096]{2,1,0:T(8,128)(2,1)S(1)}, bf16[1,256,4096]{2,1,0:T(8,128)(2,1)}, u32[]{:S(2)}) copy-start(bf16[1,256,4096]{2,1,0:T(8,128)(2,1)} %param.8) | copy-start | bytes 6291460
  82.3 66.5 %copy-start.1 = (bf16[1,256,512]{2,1,0:T(8,128)(2,1)S(1)}, bf16[1,256,512]{2,1,0:T(8,128)(2,1)}, u32[]{:S(2)}) copy-start(bf16[1,256,512]{2,1,0:T(8,128)(2,1)} %param.9) | copy-start | bytes 786436
  82.3 66.5 %copy-start.2 = (bf16[1,256,512]{2,1,0:T(8,128)(2,1)S(1)}, bf16[1,256,512]{2,1,0:T(8,128)(2,1)}, u32[]{:S(2)}) copy-start(bf16[1,256,512]{2,1,0:T(8,128)(2,1)} %param.10) | copy-start | bytes 786436

commit v2 on v1

--- a/solution.py
+++ b/solution.py
@@ -14,38 +14,81 @@
 LOW = -1e30
 
 
-def spread_kernel(keys_ref, values_ref, out_ref, sems):
-    _, heads, _, groups, _, _ = out_ref.shape
-    copies = []
+CUTS = 4
+
+
+def spread_kernel(
+    me_ref, parent_ref, len_ref, leaf_ref, keys_ref, values_ref, out_ref, table_ref,
+    rows_scr, out_scr, in_sems, out_sems,
+):
+    _, tok, width = rows_scr.shape
+    blocks, heads = tok // BLK, width // HEAD_DIM // 2
+    part, chunk = tok // CUTS, 2 * blocks
+    loads = []
     for kv, ref in enumerate((keys_ref, values_ref)):
-        for group in range(groups):
-            for j in range(heads):
-                col = (group * heads + j) * HEAD_DIM
-                copies.append(
-                    pltpu.make_async_copy(
-                        ref.at[:, :, col:col + HEAD_DIM],
-                        out_ref.at[kv, j, :, group],
-                        sems.at[len(copies)],
-                    )
+        for c in range(CUTS):
+            here = pl.ds(c * part, part)
+            loads.append(
+                pltpu.make_async_copy(ref.at[here], rows_scr.at[kv, here], in_sems.at[kv * CUTS + c])
+            )
+    for load in loads:
+        load.start()
+
+    nodes = table_ref.shape[0] * table_ref.shape[1] // 4
+    spot = lax.broadcasted_iota(jnp.int32, table_ref.shape, 0) * table_ref.shape[1]
+    spot = spot + lax.broadcasted_iota(jnp.int32, table_ref.shape, 1) - me_ref[0]
+    table = jnp.zeros(table_ref.shape, jnp.int32)
+    for at, ref in enumerate((parent_ref, len_ref, leaf_ref)):
+        table = jnp.where(spot == at * nodes, ref[0], table)
+    table_ref[...] = table
+
+    stores = []
+    for kv in range(2):
+        for c in range(CUTS):
+            loads[kv * CUTS + c].wait()
+        for j in range(heads):
+            first = (kv * heads + j) * chunk
+            for b in range(blocks):
+                for group in range(2):
+                    col = group * heads + j
+                    out_scr[first + 2 * b + group] = rows_scr[
+                        kv, b * BLK:(b + 1) * BLK, col * HEAD_DIM:(col + 1) * HEAD_DIM
+                    ]
+            here = pl.ds(first, chunk)
+            stores.append(
+                pltpu.make_async_copy(
+                    out_scr.at[here], out_ref.at[here], out_sems.at[kv * heads + j]
                 )
-    for copy in copies:
-        copy.start()
-    for copy in copies:
-        copy.wait()
-
-
-def spread(keys, values, groups):
+            )
+            stores[-1].start()
+    for store in stores:
+        store.wait()
+
+
+def spread(me, parents, node_len, req_leaf, keys, values, count):
     tok, width = keys.shape
-    blocks, heads = tok // BLK, width // HEAD_DIM // groups
-    out = pl.pallas_call(
+    pieces = 2 * (tok // BLK) * (width // HEAD_DIM)
+    heads = width // HEAD_DIM // 2
+    return pl.pallas_call(
         spread_kernel,
-        out_shape=jax.ShapeDtypeStruct((2, heads, blocks, groups, BLK, HEAD_DIM), keys.dtype),
-        in_specs=[pl.BlockSpec(memory_space=pl.ANY)] * 2,
-        out_specs=pl.BlockSpec(memory_space=pl.ANY),
-        scratch_shapes=[pltpu.SemaphoreType.DMA((2 * groups * heads,))],
+        out_shape=(
+            jax.ShapeDtypeStruct((pieces, BLK, HEAD_DIM), keys.dtype),
+            jax.ShapeDtypeStruct((4 * count // 128, 128), jnp.int32),
+        ),
+        in_specs=[pl.BlockSpec(memory_space=pltpu.SMEM)] * 4
+        + [pl.BlockSpec(memory_space=pl.ANY)] * 2,
+        out_specs=(
+            pl.BlockSpec(memory_space=pl.ANY),
+            pl.BlockSpec(memory_space=pltpu.VMEM),
+        ),
+        scratch_shapes=[
+            pltpu.VMEM((2, tok, width), keys.dtype),
+            pltpu.VMEM((pieces, BLK, HEAD_DIM), keys.dtype),
+            pltpu.SemaphoreType.DMA((2 * CUTS,)),
+            pltpu.SemaphoreType.DMA((2 * heads,)),
+        ],
         compiler_params=pltpu.CompilerParams(vmem_limit_bytes=60 << 20),
-    )(keys.reshape(blocks, BLK, width), values.reshape(blocks, BLK, width))
-    return out.reshape(-1, BLK, HEAD_DIM)
+    )(me, parents, node_len, req_leaf, keys, values)
 
 
 def pick_kernel(reqs_step, table_ref, pieces_ref, out_ref):
@@ -163,23 +206,16 @@
     )(table, me, queries, suffix_keys, suffix_values, prefix, prefix)
 
 
-def share_ints(parents, node_len, req_leaf):
-    axes = ("req", "head")
-    count = lax.axis_size("req") * lax.axis_size("head")
-    me = lax.axis_index("req") * lax.axis_size("head") + lax.axis_index("head")
-    slots = jnp.arange(count, dtype=jnp.int32) == me
-    zero = jnp.zeros((count,), jnp.int32)
-    table = jnp.concatenate(
-        [jnp.where(slots, x[0], 0) for x in (parents, node_len, req_leaf)] + [zero]
-    )
-    table = table.reshape(-1, 128)
+def share_ints(table, count):
     for bits in ((0, 1), (5, 6), (7,), (3, 4), (2,)):
         flips = [0]
         for bit in bits:
             flips += [flip | 1 << bit for flip in flips]
         total = table
         for flip in flips[1:]:
-            total = total + lax.ppermute(table, axes, [(i, i ^ flip) for i in range(count)])
+            total = total + lax.ppermute(
+                table, ("req", "head"), [(i, i ^ flip) for i in range(count)]
+            )
         table = total
     return table.reshape(-1)
 
@@ -187,13 +223,16 @@
 def per_device(
     queries, suffix_keys, suffix_values, node_keys, node_values, parents, node_len, req_leaf
 ):
-    reqs = lax.axis_size("req")
-    sent = spread(node_keys[0], node_values[0], lax.axis_size("head"))
+    reqs, groups = lax.axis_size("req"), lax.axis_size("head")
+    me = lax.axis_index("req").reshape(1)
+    flat = me * groups + lax.axis_index("head")
+    sent, table = spread(
+        flat, parents, node_len, req_leaf, node_keys[0], node_values[0], reqs * groups
+    )
     pieces = lax.all_to_all(sent, ("req", "head"), split_axis=0, concat_axis=0, tiled=True)
-    table = share_ints(parents, node_len, req_leaf)
+    table = share_ints(table, reqs * groups)
     picked = pick(table, pieces, reqs)
     prefix = lax.all_to_all(picked, "req", split_axis=0, concat_axis=0, tiled=True)
-    me = lax.axis_index("req").reshape(1)
     out = attend(table, me, queries[0], suffix_keys[0], suffix_values[0], prefix)
     return out[None]
 

time: 165 us -> 135 us (0.82)
  Pallas kernels: 50.3 us -> 20.1 us
    pallas_call x1, Pallas kernels: 33 us -> 2.82 us  [spread(): pl.pallas_call(spread_kernel, out_shape=(jax.ShapeDtypeStruct((pieces, BL...]
where the time goes in v2:
time: 135 us; the launch traced here: 134 us
  blocking collectives  65.8 us (49%)
  starting transfers between devices  32.6 us (24%)
  Pallas kernels  20.1 us (15%)
  waiting for transfers between devices  13.9 us (10%)
  between operations  2.03 us (2%)
    all_to_all x1, blocking collectives, per_device(): lax.all_to_all(picked, 'req', split_axis=0, concat_axis=0, tiled=True)  65.8 us
    ppermute x11, starting transfers between devices, share_ints(): lax.ppermute(table, ('req', 'head'), [(i, i ^ flip) for i in range(count)])  17 us
    pallas_call x1, Pallas kernels, attend(): pl.pallas_call(attend_kernel, out_shape=jax.ShapeDtypeStruct((suf, width)...  16 us
    all_to_all x1, starting transfers between devices, per_device(): lax.all_to_all(sent, ('req', 'head'), split_axis=0, concat_axis=0, tiled=...  15.7 us
    ppermute x11, waiting for transfers between devices, share_ints(): lax.ppermute(table, ('req', 'head'), [(i, i ^ flip) for i in range(count)])  13.8 us
    pallas_call x1, Pallas kernels, spread(): pl.pallas_call(spread_kernel, out_shape=(jax.ShapeDtypeStruct((pieces, BL...  2.82 us
  transfers between devices with their start and end apart: 12, of which 7 were waited for; matrix products, arithmetic and copies ran while one was open for 0% of the time, Pallas kernels for 0%

profile of v2, /device:TPU:1, one launch (start us, length us, event | category | flops | bytes accessed | tf_op | source)
XLA Modules:
  0.0 134.5 jit_solution(6890487481646747348)
XLA Ops:
  1.9 2.8 %shard_map.82 = (bf16[256,16,128]{2,1,0:T(8,128)(2,1)}, s32[8,128]{1,0:T(8,128)}) custom-call(s32[1]{0:T(128)S(6)} %add.40.me_ref, s32[1]{0:T(128)S(6)} %copy.9.parent_ref, s32[1]{0:T(128)S(6)} %copy.10.len_ref, s32[1]{0:T(128)S(6)} %copy.11.leaf_ref, bf16[256,1024]{1,0:T(8,128)(2,1)} %bitcast.13, bf16[256,1024]{1,0:T(8,128)(2,1)} %bitcast.14), custom_call_target="tpu_custom_call" | custom-call | tf_op jit(solution)/shard_map/pallas_call | solution.py:72
  4.8 0.0 copy-start.3
  4.8 15.7 %all-to-all-start = ((bf16[256,16,128]{2,1,0:T(8,128)(2,1)}), bf16[256,16,128]{2,1,0:T(8,128)(2,1)S(1)}, u32[]{:S(2)}, u32[]{:S(2)}) async-start(bf16[256,16,128]{2,1,0:T(8,128)(2,1)} %get-tuple-element.8), calls=%async_computation | async-start | bytes 2097152 | tf_op jit(solution)/shard_map/all_to_all | solution.py:232
  20.5 0.0 copy-done.3
  20.5 1.7 %collective-permute-start.2 = (s32[8,128]{1,0:T(8,128)S(1)}, s32[8,128]{1,0:T(8,128)S(1)}, u32[]{:S(2)}, u32[]{:S(2)}) collective-permute-start(s32[8,128]{1,0:T(8,128)S(1)} %copy-done.3), channel_id=1, source_target_pairs={{0,3},{1,2},{2,1},{3,0},{4,7},{5,6},{6,5},{7,4},{8,11},{9,10},{10,... | collective-permute-start | bytes 12296 | tf_op jit(solution)/shard_map/ppermute | solution.py:216
  22.2 0.6 collective-permute-start.1
  22.8 1.3 collective-permute-start
  24.1 0.0 collective-permute-done.2
  24.1 0.0 collective-permute-done.1
  24.1 1.8 %collective-permute-done = s32[8,128]{1,0:T(8,128)S(1)} collective-permute-done((s32[8,128]{1,0:T(8,128)S(1)}, s32[8,128]{1,0:T(8,128)S(1)}, u32[]{:S(2)}, u32[]{:S(2)}) %collective-permute-start) | collective-permute-done | bytes 4128 | tf_op jit(solution)/shard_map/ppermute | solution.py:216
  25.9 1.8 %collective-permute-start.5 = (s32[8,128]{1,0:T(8,128)S(1)}, s32[8,128]{1,0:T(8,128)S(1)}, u32[]{:S(2)}, u32[]{:S(2)}) collective-permute-start(s32[8,128]{1,0:T(8,128)S(1)} %add_add_fusion.2), channel_id=1, source_target_pairs={{0,96},{1,97},{2,98},{3,99},{4,100},{5,101},{6,102},{7,103},{8,104... | collective-permute-start | bytes 12296 | tf_op jit(solution)/shard_map/ppermute | solution.py:216
  27.7 0.4 collective-permute-start.4
  28.1 1.0 collective-permute-start.3
  29.1 0.7 collective-permute-done.5
  29.9 2.1 %collective-permute-done.4 = s32[8,128]{1,0:T(8,128)S(1)} collective-permute-done((s32[8,128]{1,0:T(8,128)S(1)}, s32[8,128]{1,0:T(8,128)S(1)}, u32[]{:S(2)}, u32[]{:S(2)}) %collective-permute-start.4) | collective-permute-done | bytes 4128 | tf_op jit(solution)/shard_map/ppermute | solution.py:216
  32.0 0.0 collective-permute-done.3
  32.0 2.6 %collective-permute-start.6 = (s32[8,128]{1,0:T(8,128)S(1)}, s32[8,128]{1,0:T(8,128)S(1)}, u32[]{:S(2)}, u32[]{:S(2)}) collective-permute-start(s32[8,128]{1,0:T(8,128)S(1)} %add_add_fusion.1), channel_id=1, source_target_pairs={{0,128},{1,129},{2,130},{3,131},{4,132},{5,133},{6,134},{7,135},{8... | collective-permute-start | bytes 12296 | tf_op jit(solution)/shard_map/ppermute | solution.py:216
  34.6 1.8 %collective-permute-done.6 = s32[8,128]{1,0:T(8,128)S(1)} collective-permute-done((s32[8,128]{1,0:T(8,128)S(1)}, s32[8,128]{1,0:T(8,128)S(1)}, u32[]{:S(2)}, u32[]{:S(2)}) %collective-permute-start.6) | collective-permute-done | bytes 4128 | tf_op jit(solution)/shard_map/ppermute | solution.py:216
  36.3 4.8 %collective-permute-start.9 = (s32[8,128]{1,0:T(8,128)S(1)}, s32[8,128]{1,0:T(8,128)S(1)}, u32[]{:S(2)}, u32[]{:S(2)}) collective-permute-start(s32[8,128]{1,0:T(8,128)S(1)} %add.47), channel_id=1, source_target_pairs={{0,24},{1,25},{2,26},{3,27},{4,28},{5,29},{6,30},{7,31},{8,16},{9,... | collective-permute-start | bytes 12296 | tf_op jit(solution)/shard_map/ppermute | solution.py:216
  41.1 1.2 collective-permute-start.8
  42.3 0.9 collective-permute-start.7
  43.2 2.9 %collective-permute-done.9 = s32[8,128]{1,0:T(8,128)S(1)} collective-permute-done((s32[8,128]{1,0:T(8,128)S(1)}, s32[8,128]{1,0:T(8,128)S(1)}, u32[]{:S(2)}, u32[]{:S(2)}) %collective-permute-start.9) | collective-permute-done | bytes 4128 | tf_op jit(solution)/shard_map/ppermute | solution.py:216
  46.1 2.4 %collective-permute-done.8 = s32[8,128]{1,0:T(8,128)S(1)} collective-permute-done((s32[8,128]{1,0:T(8,128)S(1)}, s32[8,128]{1,0:T(8,128)S(1)}, u32[]{:S(2)}, u32[]{:S(2)}) %collective-permute-start.8) | collective-permute-done | bytes 4128 | tf_op jit(solution)/shard_map/ppermute | solution.py:216
  48.5 0.0 collective-permute-done.7
  48.5 0.7 collective-permute-start.10
  49.1 2.2 %collective-permute-done.10 = s32[8,128]{1,0:T(8,128)S(1)} collective-permute-done((s32[8,128]{1,0:T(8,128)S(1)}, s32[8,128]{1,0:T(8,128)S(1)}, u32[]{:S(2)}, u32[]{:S(2)}) %collective-permute-start.10) | collective-permute-done | bytes 4128 | tf_op jit(solution)/shard_map/ppermute | solution.py:216
  51.3 0.0 all-to-all-done.pieces_ref
  51.3 1.3 shard_map.83
  52.6 0.0 copy-start
  52.7 0.0 copy-start.1
  52.7 0.0 copy-start.2
  52.7 65.8 %all_to_all.10.pk_ref.pv_ref = bf16[128,64,128]{2,1,0:T(8,128)(2,1)S(1)} all-to-all(bf16[128,64,128]{2,1,0:T(8,128)(2,1)S(1)} %shard_map.83), channel_id=1, replica_groups=mesh['req'=128,'head'=2] {'req'}, dimensions={0} | all-to-all | bytes 4194304 | tf_op jit(solution)/shard_map/all_to_all | solution.py:235
  118.5 0.0 copy-done
  118.5 0.0 copy-done.1
  118.5 0.0 copy-done.2
  118.5 16.0 %shard_map.84 = bf16[256,4096]{1,0:T(8,128)(2,1)} custom-call(s32[1024]{0:T(1024)S(1)} %add_bitcast_fusion.table_ref, s32[1]{0:T(128)} %bitcast.me_ref, bf16[256,4096]{1,0:T(8,128)(2,1)S(1)} %bitcast.10, bf16[256,512]{1,0:T(8,128)(2,1)S(1)} %bitcast.11, bf16[256,512]{1,0:T(8,128)(2,1)S(1)} %bitcast.12, bf16[128,64,128]{2,1,0:T(8,128)(2,1)S(1)} %all_to_all.10.pk_ref.pv_ref, ...), custom_call_target="tpu_custom_call" | custom-call | tf_op jit(solution)/shard_map/pallas_call | solution.py:185
  (5 shorter events, 0.0 us)
Async XLA Ops:
  4.8 15.7 %copy-start.3 = (s32[8,128]{1,0:T(8,128)S(1)}, s32[8,128]{1,0:T(8,128)}, u32[]{:S(2)}) copy-start(s32[8,128]{1,0:T(8,128)} %get-tuple-element.7) | copy-start | bytes 12292
  4.8 46.5 %all-to-all-start = ((bf16[256,16,128]{2,1,0:T(8,128)(2,1)}), bf16[256,16,128]{2,1,0:T(8,128)(2,1)S(1)}, u32[]{:S(2)}, u32[]{:S(2)}) async-start(bf16[256,16,128]{2,1,0:T(8,128)(2,1)} %get-tuple-element.8), calls=%async_computation | async-start | bytes 2097152 | tf_op jit(solution)/shard_map/all_to_all | solution.py:232
  20.5 3.6 %collective-permute-start.2 = (s32[8,128]{1,0:T(8,128)S(1)}, s32[8,128]{1,0:T(8,128)S(1)}, u32[]{:S(2)}, u32[]{:S(2)}) collective-permute-start(s32[8,128]{1,0:T(8,128)S(1)} %copy-done.3), channel_id=1, source_target_pairs={{0,3},{1,2},{2,1},{3,0},{4,7},{5,6},{6,5},{7,4},{8,11},{9,10},{10,... | collective-permute-start | bytes 12296 | tf_op jit(solution)/shard_map/ppermute | solution.py:216
  22.2 1.9 %collective-permute-start.1 = (s32[8,128]{1,0:T(8,128)S(1)}, s32[8,128]{1,0:T(8,128)S(1)}, u32[]{:S(2)}, u32[]{:S(2)}) collective-permute-start(s32[8,128]{1,0:T(8,128)S(1)} %copy-done.3), channel_id=1, source_target_pairs={{0,2},{1,3},{2,0},{3,1},{4,6},{5,7},{6,4},{7,5},{8,10},{9,11},{10,... | collective-permute-start | bytes 12296 | tf_op jit(solution)/shard_map/ppermute | solution.py:216
  22.8 3.1 %collective-permute-start = (s32[8,128]{1,0:T(8,128)S(1)}, s32[8,128]{1,0:T(8,128)S(1)}, u32[]{:S(2)}, u32[]{:S(2)}) collective-permute-start(s32[8,128]{1,0:T(8,128)S(1)} %copy-done.3), channel_id=1, source_target_pairs={{0,1},{1,0},{2,3},{3,2},{4,5},{5,4},{6,7},{7,6},{8,9},{9,8},{10,11... | collective-permute-start | bytes 12296 | tf_op jit(solution)/shard_map/ppermute | solution.py:216
  25.9 4.0 %collective-permute-start.5 = (s32[8,128]{1,0:T(8,128)S(1)}, s32[8,128]{1,0:T(8,128)S(1)}, u32[]{:S(2)}, u32[]{:S(2)}) collective-permute-start(s32[8,128]{1,0:T(8,128)S(1)} %add_add_fusion.2), channel_id=1, source_target_pairs={{0,96},{1,97},{2,98},{3,99},{4,100},{5,101},{6,102},{7,103},{8,104... | collective-permute-start | bytes 12296 | tf_op jit(solution)/shard_map/ppermute | solution.py:216
  27.7 4.3 %collective-permute-start.4 = (s32[8,128]{1,0:T(8,128)S(1)}, s32[8,128]{1,0:T(8,128)S(1)}, u32[]{:S(2)}, u32[]{:S(2)}) collective-permute-start(s32[8,128]{1,0:T(8,128)S(1)} %add_add_fusion.2), channel_id=1, source_target_pairs={{0,64},{1,65},{2,66},{3,67},{4,68},{5,69},{6,70},{7,71},{8,72},{9,... | collective-permute-start | bytes 12296 | tf_op jit(solution)/shard_map/ppermute | solution.py:216
  28.1 3.9 %collective-permute-start.3 = (s32[8,128]{1,0:T(8,128)S(1)}, s32[8,128]{1,0:T(8,128)S(1)}, u32[]{:S(2)}, u32[]{:S(2)}) collective-permute-start(s32[8,128]{1,0:T(8,128)S(1)} %add_add_fusion.2), channel_id=1, source_target_pairs={{0,32},{1,33},{2,34},{3,35},{4,36},{5,37},{6,38},{7,39},{8,40},{9,... | collective-permute-start | bytes 12296 | tf_op jit(solution)/shard_map/ppermute | solution.py:216
  32.0 4.3 %collective-permute-start.6 = (s32[8,128]{1,0:T(8,128)S(1)}, s32[8,128]{1,0:T(8,128)S(1)}, u32[]{:S(2)}, u32[]{:S(2)}) collective-permute-start(s32[8,128]{1,0:T(8,128)S(1)} %add_add_fusion.1), channel_id=1, source_target_pairs={{0,128},{1,129},{2,130},{3,131},{4,132},{5,133},{6,134},{7,135},{8... | collective-permute-start | bytes 12296 | tf_op jit(solution)/shard_map/ppermute | solution.py:216
  36.3 9.7 %collective-permute-start.9 = (s32[8,128]{1,0:T(8,128)S(1)}, s32[8,128]{1,0:T(8,128)S(1)}, u32[]{:S(2)}, u32[]{:S(2)}) collective-permute-start(s32[8,128]{1,0:T(8,128)S(1)} %add.47), channel_id=1, source_target_pairs={{0,24},{1,25},{2,26},{3,27},{4,28},{5,29},{6,30},{7,31},{8,16},{9,... | collective-permute-start | bytes 12296 | tf_op jit(solution)/shard_map/ppermute | solution.py:216
  41.1 7.4 %collective-permute-start.8 = (s32[8,128]{1,0:T(8,128)S(1)}, s32[8,128]{1,0:T(8,128)S(1)}, u32[]{:S(2)}, u32[]{:S(2)}) collective-permute-start(s32[8,128]{1,0:T(8,128)S(1)} %add.47), channel_id=1, source_target_pairs={{0,16},{1,17},{2,18},{3,19},{4,20},{5,21},{6,22},{7,23},{8,24},{9,... | collective-permute-start | bytes 12296 | tf_op jit(solution)/shard_map/ppermute | solution.py:216
  42.3 6.2 %collective-permute-start.7 = (s32[8,128]{1,0:T(8,128)S(1)}, s32[8,128]{1,0:T(8,128)S(1)}, u32[]{:S(2)}, u32[]{:S(2)}) collective-permute-start(s32[8,128]{1,0:T(8,128)S(1)} %add.47), channel_id=1, source_target_pairs={{0,8},{1,9},{2,10},{3,11},{4,12},{5,13},{6,14},{7,15},{8,0},{9,1},... | collective-permute-start | bytes 12296 | tf_op jit(solution)/shard_map/ppermute | solution.py:216
  48.5 2.8 %collective-permute-start.10 = (s32[8,128]{1,0:T(8,128)S(1)}, s32[8,128]{1,0:T(8,128)S(1)}, u32[]{:S(2)}, u32[]{:S(2)}) collective-permute-start(s32[8,128]{1,0:T(8,128)S(1)} %add_add_fusion), channel_id=1, source_target_pairs={{0,4},{1,5},{2,6},{3,7},{4,0},{5,1},{6,2},{7,3},{8,12},{9,13},{10,... | collective-permute-start | bytes 12296 | tf_op jit(solution)/shard_map/ppermute | solution.py:216
  52.6 65.9 %copy-start = (bf16[1,256,4096]{2,1,0:T(8,128)(2,1)S(1)}, bf16[1,256,4096]{2,1,0:T(8,128)(2,1)}, u32[]{:S(2)}) copy-start(bf16[1,256,4096]{2,1,0:T(8,128)(2,1)} %param.8) | copy-start | bytes 6291460
  52.7 65.8 %copy-start.1 = (bf16[1,256,512]{2,1,0:T(8,128)(2,1)S(1)}, bf16[1,256,512]{2,1,0:T(8,128)(2,1)}, u32[]{:S(2)}) copy-start(bf16[1,256,512]{2,1,0:T(8,128)(2,1)} %param.9) | copy-start | bytes 786436
  52.7 65.8 %copy-start.2 = (bf16[1,256,512]{2,1,0:T(8,128)(2,1)S(1)}, bf16[1,256,512]{2,1,0:T(8,128)(2,1)}, u32[]{:S(2)}) copy-start(bf16[1,256,512]{2,1,0:T(8,128)(2,1)} %param.10) | copy-start | bytes 786436

commit v3 on v2

v3 whole, which is shorter than its diff:
```python
import functools
import math

import jax
import jax.numpy as jnp
from jax import lax
from jax.experimental import pallas as pl
from jax.experimental.pallas import tpu as pltpu
from jax.sharding import PartitionSpec as P

HEAD_DIM = 128
DEPTH = 4
BLK = 16
LOW = -1e30


CUTS = 4


def spread_kernel(
    parent_ref, len_ref, leaf_ref, keys_ref, values_ref, out_ref, table_ref,
    rows_scr, out_scr, in_sems, out_sems,
):
    _, tok, width = rows_scr.shape
    blocks, heads = tok // BLK, width // HEAD_DIM // 2
    part, chunk = tok // CUTS, 2 * blocks
    loads = []
    for kv, ref in enumerate((keys_ref, values_ref)):
        for c in range(CUTS):
            here = pl.ds(c * part, part)
            loads.append(
                pltpu.make_async_copy(ref.at[here], rows_scr.at[kv, here], in_sems.at[kv * CUTS + c])
            )
    for load in loads:
        load.start()

    stores = []
    for kv in range(2):
        for c in range(CUTS):
            loads[kv * CUTS + c].wait()
        for j in range(heads):
            first = (kv * heads + j) * chunk
            for b in range(blocks):
                for group in range(2):
                    col = group * heads + j
                    out_scr[first + 2 * b + group] = rows_scr[
                        kv, b * BLK:(b + 1) * BLK, col * HEAD_DIM:(col + 1) * HEAD_DIM
                    ]
            here = pl.ds(first, chunk)
            stores.append(
                pltpu.make_async_copy(
                    out_scr.at[here], out_ref.at[here], out_sems.at[kv * heads + j]
                )
            )
            stores[-1].start()
    me = lax.axis_index("req") * lax.axis_size("head") + lax.axis_index("head")
    nodes = table_ref.shape[0] * table_ref.shape[1] // 4
    spot = lax.broadcasted_iota(jnp.int32, table_ref.shape, 0) * table_ref.shape[1]
    spot = spot + lax.broadcasted_iota(jnp.int32, table_ref.shape, 1) - me
    table = jnp.zeros(table_ref.shape, jnp.int32)
    for i, ref in enumerate((parent_ref, len_ref, leaf_ref)):
        table = jnp.where(spot == i * nodes, ref[...], table)
    table_ref[...] = table

    for store in stores:
        store.wait()


def spread(parents, node_len, req_leaf, keys, values, count):
    tok, width = keys.shape
    pieces = 2 * (tok // BLK) * (width // HEAD_DIM)
    heads = width // HEAD_DIM // 2
    return pl.pallas_call(
        spread_kernel,
        out_shape=(
            jax.ShapeDtypeStruct((pieces, BLK, HEAD_DIM), keys.dtype),
            jax.ShapeDtypeStruct((4 * count // 128, 128), jnp.int32),
        ),
        in_specs=[pl.BlockSpec(memory_space=pltpu.VMEM)] * 3
        + [pl.BlockSpec(memory_space=pl.ANY)] * 2,
        out_specs=(
            pl.BlockSpec(memory_space=pl.ANY),
            pl.BlockSpec(memory_space=pltpu.VMEM),
        ),
        scratch_shapes=[
            pltpu.VMEM((2, tok, width), keys.dtype),
            pltpu.VMEM((pieces, BLK, HEAD_DIM), keys.dtype),
            pltpu.SemaphoreType.DMA((2 * CUTS,)),
            pltpu.SemaphoreType.DMA((2 * heads,)),
        ],
        compiler_params=pltpu.CompilerParams(vmem_limit_bytes=60 << 20),
    )(*(x.reshape(1, 1) for x in (parents, node_len, req_leaf)), keys, values)


def pick_kernel(reqs_step, table_ref, pieces_ref, out_ref):
    nodes = pieces_ref.shape[0]
    base = pl.program_id(0) * reqs_step

    def one(r, carry):
        node = table_ref[2 * nodes + 2 * (base + r)]
        for i in range(DEPTH):
            out_ref[r, i * BLK:(i + 1) * BLK, :] = pieces_ref[node]
            if i < DEPTH - 1:
                node = table_ref[node]
        return carry

    lax.fori_loop(0, reqs_step, one, 0, unroll=8)


def pick(table, pieces, reqs):
    steps = 4
    reqs_step = reqs // steps
    return pl.pallas_call(
        functools.partial(pick_kernel, reqs_step),
        out_shape=jax.ShapeDtypeStruct((reqs, DEPTH * BLK, HEAD_DIM), pieces.dtype),
        grid_spec=pltpu.PrefetchScalarGridSpec(
            num_scalar_prefetch=1,
            grid=(steps,),
            in_specs=[pl.BlockSpec(pieces.shape, lambda s, t: (0, 0, 0))],
            out_specs=pl.BlockSpec((reqs_step, DEPTH * BLK, HEAD_DIM), lambda s, t: (s, 0, 0)),
        ),
        compiler_params=pltpu.CompilerParams(vmem_limit_bytes=32 << 20),
    )(table, pieces)


FACTOR = math.log2(math.e) / math.sqrt(HEAD_DIM)
OVER = (((1,), (1,)), ((), ()))


def attend_kernel(
    table_ref, query_ref, sk_ref, sv_ref, prefix_ref, out_ref,
    key_scr, val_scr, out_scr, sems,
):
    nodes = table_ref.shape[0] // 4
    suf = sk_ref.shape[0]
    heads = sk_ref.shape[1] // HEAD_DIM
    blocks, rows = prefix_ref.shape[0] // (2 * heads), prefix_ref.shape[1]
    cached = blocks * rows
    group = query_ref.shape[1] // HEAD_DIM // heads

    node = table_ref[2 * nodes + 2 * lax.axis_index("req")]
    spans = []
    for i in range(DEPTH):
        spans.append(table_ref[nodes + node])
        if i < DEPTH - 1:
            node = table_ref[node]
    shape = (blocks, BLK, HEAD_DIM)
    tok = lax.broadcasted_iota(jnp.int32, shape, 0) * BLK
    tok = tok + lax.broadcasted_iota(jnp.int32, shape, 1)
    seen = [tok < span for span in spans]
    row = lax.broadcasted_iota(jnp.int32, (suf, suf), 0)
    causal = row >= lax.broadcasted_iota(jnp.int32, (suf, suf), 1)

    shown = jnp.stack([x.astype(jnp.float32).astype(jnp.bfloat16) for x in seen], axis=1)
    shown = shown.reshape(cached, HEAD_DIM)
    for slot in range(val_scr.shape[0]):
        val_scr[slot, :cached, HEAD_DIM:] = shown
        val_scr[slot, cached:, HEAD_DIM:] = jnp.ones((suf, HEAD_DIM), val_scr.dtype)

    def prepare(j):
        slot = j % val_scr.shape[0]
        keys, values = [], []
        for i in range(DEPTH):
            here = slice(i * BLK, (i + 1) * BLK)
            key = prefix_ref[j * blocks:(j + 1) * blocks, here, :].astype(jnp.float32)
            keys.append(jnp.where(seen[i], key, key[:1, :1]).astype(jnp.bfloat16))
            value = prefix_ref[(heads + j) * blocks:(heads + j + 1) * blocks, here, :]
            values.append(jnp.where(seen[i], value.astype(jnp.float32), 0.0).astype(jnp.bfloat16))
        own = slice(j * HEAD_DIM, (j + 1) * HEAD_DIM)
        key_scr[slot, :cached] = jnp.stack(keys, axis=1).reshape(cached, HEAD_DIM)
        val_scr[slot, :cached, :HEAD_DIM] = jnp.stack(values, axis=1).reshape(cached, HEAD_DIM)
        key_scr[slot, cached:] = sk_ref[:, own]
        val_scr[slot, cached:, :HEAD_DIM] = sv_ref[:, own]

    def scores_of(item):
        j = item // group
        if item % group == 0:
            prepare(j)
        query = query_ref[:, item * HEAD_DIM:(item + 1) * HEAD_DIM]
        return lax.dot_general(
            query, key_scr[j % key_scr.shape[0]], OVER, preferred_element_type=jnp.float32
        )

    stores = []
    for item in range(heads * group):
        j, g = divmod(item, group)
        scores = scores_of(item)
        old, new = scores[:, :cached], jnp.where(causal, scores[:, cached:], LOW)
        top = jnp.maximum(
            jnp.max(old, axis=1, keepdims=True), jnp.max(new, axis=1, keepdims=True)
        )
        weights = jnp.concatenate(
            [jnp.exp2((x - top) * FACTOR).astype(jnp.bfloat16) for x in (old, new)], axis=1
        )
        sums = jnp.dot(
            weights, val_scr[j % val_scr.shape[0]], preferred_element_type=jnp.float32
        )
        attended = sums[:, :HEAD_DIM] / sums[:, HEAD_DIM:]
        out_scr[j, :, g * HEAD_DIM:(g + 1) * HEAD_DIM] = attended.astype(out_scr.dtype)
        if g == group - 1:
            at = pl.ds(j * group * HEAD_DIM, group * HEAD_DIM)
            stores.append(
                pltpu.make_async_copy(out_scr.at[j], out_ref.at[:, at], sems.at[j])
            )
            stores[-1].start()
    for store in stores:
        store.wait()


def attend(table, queries, suffix_keys, suffix_values, prefix):
    suf, width = queries.shape
    heads = suffix_keys.shape[1] // HEAD_DIM
    total = prefix.shape[0] // (2 * heads) * prefix.shape[1] + suf
    return pl.pallas_call(
        attend_kernel,
        out_shape=jax.ShapeDtypeStruct((suf, width), jnp.bfloat16),
        in_specs=[pl.BlockSpec(memory_space=pltpu.SMEM)]
        + [pl.BlockSpec(memory_space=pltpu.VMEM)] * 4,
        out_specs=pl.BlockSpec(memory_space=pl.ANY),
        scratch_shapes=[
            pltpu.VMEM((2, total, HEAD_DIM), jnp.bfloat16),
            pltpu.VMEM((2, total, 2 * HEAD_DIM), jnp.bfloat16),
            pltpu.VMEM((heads, suf, width // heads), jnp.bfloat16),
            pltpu.SemaphoreType.DMA((heads,)),
        ],
        compiler_params=pltpu.CompilerParams(vmem_limit_bytes=40 << 20),
    )(table, queries, suffix_keys, suffix_values, prefix)


def share_ints(table, count):
    for bits in ((0, 1), (5, 6), (7,), (3, 4), (2,)):
        flips = [0]
        for bit in bits:
            flips += [flip | 1 << bit for flip in flips]
        total = table
        for flip in flips[1:]:
            total = total + lax.ppermute(
                table, ("req", "head"), [(i, i ^ flip) for i in range(count)]
            )
        table = total
    return table.reshape(-1)


def per_device(
    queries, suffix_keys, suffix_values, node_keys, node_values, parents, node_len, req_leaf
):
    reqs, groups = lax.axis_size("req"), lax.axis_size("head")
    sent, table = spread(
        parents, node_len, req_leaf, node_keys[0], node_values[0], reqs * groups
    )
    pieces = lax.all_to_all(sent, ("req", "head"), split_axis=0, concat_axis=0, tiled=True)
    table = share_ints(table, reqs * groups)
    picked = pick(table, pieces, reqs)
    prefix = lax.all_to_all(picked, "req", split_axis=0, concat_axis=0, tiled=True)
    out = attend(table, queries[0], suffix_keys[0], suffix_values[0], prefix)
    return out[None]


def solution(mesh):
    in_specs = (
        P("req", None, "head"),
        P("req", None, "head"),
        P("req", None, "head"),
        P(("req", "head"), None, None),
        P(("req", "head"), None, None),
        P(("req", "head")),
        P(("req", "head")),
        P("req"),
    )
    out_specs = P("req", None, "head")
    return jax.shard_map(
        per_device, mesh=mesh, in_specs=in_specs, out_specs=out_specs, check_vma=False
    )
```

time: 135 us -> 133 us (0.985)
  Pallas kernels: 20.1 us -> 17.8 us
    pallas_call x1, Pallas kernels: 16 us -> 13.7 us  [attend(): pl.pallas_call(attend_kernel, out_shape=jax.ShapeDtypeStruct((suf, width)...]
where the time goes in v3:
time: 133 us; the launch traced here: 132 us
  blocking collectives  65.8 us (49%)
  starting transfers between devices  32.6 us (25%)
  Pallas kernels  17.8 us (13%)
  waiting for transfers between devices  13.9 us (10%)
  between operations  2.19 us (2%)
    all_to_all x1, blocking collectives, per_device(): lax.all_to_all(picked, 'req', split_axis=0, concat_axis=0, tiled=True)  65.8 us
    ppermute x11, starting transfers between devices, share_ints(): lax.ppermute(table, ('req', 'head'), [(i, i ^ flip) for i in range(count)])  17 us
    all_to_all x1, starting transfers between devices, per_device(): lax.all_to_all(sent, ('req', 'head'), split_axis=0, concat_axis=0, tiled=...  15.7 us
    ppermute x11, waiting for transfers between devices, share_ints(): lax.ppermute(table, ('req', 'head'), [(i, i ^ flip) for i in range(count)])  13.8 us
    pallas_call x1, Pallas kernels, attend(): pl.pallas_call(attend_kernel, out_shape=jax.ShapeDtypeStruct((suf, width)...  13.7 us
    pallas_call x1, Pallas kernels, spread(): pl.pallas_call(spread_kernel, out_shape=(jax.ShapeDtypeStruct((pieces, BL...  2.82 us
  transfers between devices with their start and end apart: 12, of which 7 were waited for; matrix products, arithmetic and copies ran while one was open for 0% of the time, Pallas kernels for 0%

profile of v3, /device:TPU:1, one launch (start us, length us, event | category | flops | bytes accessed | tf_op | source)
XLA Modules:
  0.0 132.3 jit_solution(16467583772957515935)
XLA Ops:
  1.9 2.8 %shard_map.82 = (bf16[256,16,128]{2,1,0:T(8,128)(2,1)}, s32[8,128]{1,0:T(8,128)}) custom-call(s32[1,1]{1,0:T(1,128)} %bitcast.11.parent_ref, s32[1,1]{1,0:T(1,128)} %bitcast.12.len_ref, s32[1,1]{1,0:T(1,128)} %bitcast.13.leaf_ref, bf16[256,1024]{1,0:T(8,128)(2,1)} %bitcast.17, bf16[256,1024]{1,0:T(8,128)(2,1)} %bitcast.18), custom_call_target="tpu_custom_call" | custom-call | tf_op jit(solution)/shard_map/pallas_call | solution.py:73
  4.8 0.0 copy-start.3
  4.8 15.7 %all-to-all-start = ((bf16[256,16,128]{2,1,0:T(8,128)(2,1)}), bf16[256,16,128]{2,1,0:T(8,128)(2,1)S(1)}, u32[]{:S(2)}, u32[]{:S(2)}) async-start(bf16[256,16,128]{2,1,0:T(8,128)(2,1)} %get-tuple-element.8), calls=%async_computation | async-start | bytes 2097152 | tf_op jit(solution)/shard_map/all_to_all | solution.py:251
  20.5 0.0 copy-done.3
  20.5 1.7 %collective-permute-start.2 = (s32[8,128]{1,0:T(8,128)S(1)}, s32[8,128]{1,0:T(8,128)S(1)}, u32[]{:S(2)}, u32[]{:S(2)}) collective-permute-start(s32[8,128]{1,0:T(8,128)S(1)} %copy-done.3), channel_id=1, source_target_pairs={{0,3},{1,2},{2,1},{3,0},{4,7},{5,6},{6,5},{7,4},{8,11},{9,10},{10,... | collective-permute-start | bytes 12296 | tf_op jit(solution)/shard_map/ppermute | solution.py:237
  22.2 0.6 collective-permute-start.1
  22.8 1.3 collective-permute-start
  24.1 0.0 collective-permute-done.2
  24.1 0.0 collective-permute-done.1
  24.1 1.8 %collective-permute-done = s32[8,128]{1,0:T(8,128)S(1)} collective-permute-done((s32[8,128]{1,0:T(8,128)S(1)}, s32[8,128]{1,0:T(8,128)S(1)}, u32[]{:S(2)}, u32[]{:S(2)}) %collective-permute-start) | collective-permute-done | bytes 4128 | tf_op jit(solution)/shard_map/ppermute | solution.py:237
  25.9 1.8 %collective-permute-start.5 = (s32[8,128]{1,0:T(8,128)S(1)}, s32[8,128]{1,0:T(8,128)S(1)}, u32[]{:S(2)}, u32[]{:S(2)}) collective-permute-start(s32[8,128]{1,0:T(8,128)S(1)} %add_add_fusion.2), channel_id=1, source_target_pairs={{0,96},{1,97},{2,98},{3,99},{4,100},{5,101},{6,102},{7,103},{8,104... | collective-permute-start | bytes 12296 | tf_op jit(solution)/shard_map/ppermute | solution.py:237
  27.7 0.4 collective-permute-start.4
  28.1 1.0 collective-permute-start.3
  29.1 0.7 collective-permute-done.5
  29.9 2.1 %collective-permute-done.4 = s32[8,128]{1,0:T(8,128)S(1)} collective-permute-done((s32[8,128]{1,0:T(8,128)S(1)}, s32[8,128]{1,0:T(8,128)S(1)}, u32[]{:S(2)}, u32[]{:S(2)}) %collective-permute-start.4) | collective-permute-done | bytes 4128 | tf_op jit(solution)/shard_map/ppermute | solution.py:237
  32.0 0.0 collective-permute-done.3
  32.0 2.6 %collective-permute-start.6 = (s32[8,128]{1,0:T(8,128)S(1)}, s32[8,128]{1,0:T(8,128)S(1)}, u32[]{:S(2)}, u32[]{:S(2)}) collective-permute-start(s32[8,128]{1,0:T(8,128)S(1)} %add_add_fusion.1), channel_id=1, source_target_pairs={{0,128},{1,129},{2,130},{3,131},{4,132},{5,133},{6,134},{7,135},{8... | collective-permute-start | bytes 12296 | tf_op jit(solution)/shard_map/ppermute | solution.py:237
  34.6 1.8 %collective-permute-done.6 = s32[8,128]{1,0:T(8,128)S(1)} collective-permute-done((s32[8,128]{1,0:T(8,128)S(1)}, s32[8,128]{1,0:T(8,128)S(1)}, u32[]{:S(2)}, u32[]{:S(2)}) %collective-permute-start.6) | collective-permute-done | bytes 4128 | tf_op jit(solution)/shard_map/ppermute | solution.py:237
  36.3 4.8 %collective-permute-start.9 = (s32[8,128]{1,0:T(8,128)S(1)}, s32[8,128]{1,0:T(8,128)S(1)}, u32[]{:S(2)}, u32[]{:S(2)}) collective-permute-start(s32[8,128]{1,0:T(8,128)S(1)} %add.39), channel_id=1, source_target_pairs={{0,24},{1,25},{2,26},{3,27},{4,28},{5,29},{6,30},{7,31},{8,16},{9,... | collective-permute-start | bytes 12296 | tf_op jit(solution)/shard_map/ppermute | solution.py:237
  41.1 1.2 collective-permute-start.8
  42.3 0.9 collective-permute-start.7
  43.2 2.9 %collective-permute-done.9 = s32[8,128]{1,0:T(8,128)S(1)} collective-permute-done((s32[8,128]{1,0:T(8,128)S(1)}, s32[8,128]{1,0:T(8,128)S(1)}, u32[]{:S(2)}, u32[]{:S(2)}) %collective-permute-start.9) | collective-permute-done | bytes 4128 | tf_op jit(solution)/shard_map/ppermute | solution.py:237
  46.1 2.4 %collective-permute-done.8 = s32[8,128]{1,0:T(8,128)S(1)} collective-permute-done((s32[8,128]{1,0:T(8,128)S(1)}, s32[8,128]{1,0:T(8,128)S(1)}, u32[]{:S(2)}, u32[]{:S(2)}) %collective-permute-start.8) | collective-permute-done | bytes 4128 | tf_op jit(solution)/shard_map/ppermute | solution.py:237
  48.5 0.0 collective-permute-done.7
  48.5 0.7 collective-permute-start.10
  49.2 2.2 %collective-permute-done.10 = s32[8,128]{1,0:T(8,128)S(1)} collective-permute-done((s32[8,128]{1,0:T(8,128)S(1)}, s32[8,128]{1,0:T(8,128)S(1)}, u32[]{:S(2)}, u32[]{:S(2)}) %collective-permute-start.10) | collective-permute-done | bytes 4128 | tf_op jit(solution)/shard_map/ppermute | solution.py:237
  51.3 0.0 all-to-all-done.pieces_ref
  51.3 1.3 shard_map.83
  52.6 0.0 copy-start
  52.7 0.0 copy-start.1
  52.7 0.0 copy-start.2
  52.7 65.8 %all_to_all.10.prefix_ref = bf16[128,64,128]{2,1,0:T(8,128)(2,1)S(1)} all-to-all(bf16[128,64,128]{2,1,0:T(8,128)(2,1)S(1)} %shard_map.83), channel_id=1, replica_groups=mesh['req'=128,'head'=2] {'req'}, dimensions={0} | all-to-all | bytes 4194304 | tf_op jit(solution)/shard_map/all_to_all | solution.py:254
  118.5 0.0 copy-done
  118.5 0.0 copy-done.1
  118.5 0.0 copy-done.2
  118.5 13.7 %shard_map.84 = bf16[256,4096]{1,0:T(8,128)(2,1)} custom-call(s32[1024]{0:T(1024)S(1)} %add_bitcast_fusion.table_ref, bf16[256,4096]{1,0:T(8,128)(2,1)S(1)} %bitcast.14, bf16[256,512]{1,0:T(8,128)(2,1)S(1)} %bitcast.15, bf16[256,512]{1,0:T(8,128)(2,1)S(1)} %bitcast.16, bf16[128,64,128]{2,1,0:T(8,128)(2,1)S(1)} %all_to_all.10.prefix_ref), custom_call_target="tpu_custom_call" | custom-call | tf_op jit(solution)/shard_map/pallas_call | solution.py:214
  (5 shorter events, 0.0 us)
Async XLA Ops:
  4.8 15.7 %copy-start.3 = (s32[8,128]{1,0:T(8,128)S(1)}, s32[8,128]{1,0:T(8,128)}, u32[]{:S(2)}) copy-start(s32[8,128]{1,0:T(8,128)} %get-tuple-element.7) | copy-start | bytes 12292
  4.8 46.5 %all-to-all-start = ((bf16[256,16,128]{2,1,0:T(8,128)(2,1)}), bf16[256,16,128]{2,1,0:T(8,128)(2,1)S(1)}, u32[]{:S(2)}, u32[]{:S(2)}) async-start(bf16[256,16,128]{2,1,0:T(8,128)(2,1)} %get-tuple-element.8), calls=%async_computation | async-start | bytes 2097152 | tf_op jit(solution)/shard_map/all_to_all | solution.py:251
  20.5 3.6 %collective-permute-start.2 = (s32[8,128]{1,0:T(8,128)S(1)}, s32[8,128]{1,0:T(8,128)S(1)}, u32[]{:S(2)}, u32[]{:S(2)}) collective-permute-start(s32[8,128]{1,0:T(8,128)S(1)} %copy-done.3), channel_id=1, source_target_pairs={{0,3},{1,2},{2,1},{3,0},{4,7},{5,6},{6,5},{7,4},{8,11},{9,10},{10,... | collective-permute-start | bytes 12296 | tf_op jit(solution)/shard_map/ppermute | solution.py:237
  22.2 1.9 %collective-permute-start.1 = (s32[8,128]{1,0:T(8,128)S(1)}, s32[8,128]{1,0:T(8,128)S(1)}, u32[]{:S(2)}, u32[]{:S(2)}) collective-permute-start(s32[8,128]{1,0:T(8,128)S(1)} %copy-done.3), channel_id=1, source_target_pairs={{0,2},{1,3},{2,0},{3,1},{4,6},{5,7},{6,4},{7,5},{8,10},{9,11},{10,... | collective-permute-start | bytes 12296 | tf_op jit(solution)/shard_map/ppermute | solution.py:237
  22.8 3.1 %collective-permute-start = (s32[8,128]{1,0:T(8,128)S(1)}, s32[8,128]{1,0:T(8,128)S(1)}, u32[]{:S(2)}, u32[]{:S(2)}) collective-permute-start(s32[8,128]{1,0:T(8,128)S(1)} %copy-done.3), channel_id=1, source_target_pairs={{0,1},{1,0},{2,3},{3,2},{4,5},{5,4},{6,7},{7,6},{8,9},{9,8},{10,11... | collective-permute-start | bytes 12296 | tf_op jit(solution)/shard_map/ppermute | solution.py:237
  25.9 4.0 %collective-permute-start.5 = (s32[8,128]{1,0:T(8,128)S(1)}, s32[8,128]{1,0:T(8,128)S(1)}, u32[]{:S(2)}, u32[]{:S(2)}) collective-permute-start(s32[8,128]{1,0:T(8,128)S(1)} %add_add_fusion.2), channel_id=1, source_target_pairs={{0,96},{1,97},{2,98},{3,99},{4,100},{5,101},{6,102},{7,103},{8,104... | collective-permute-start | bytes 12296 | tf_op jit(solution)/shard_map/ppermute | solution.py:237
  27.7 4.3 %collective-permute-start.4 = (s32[8,128]{1,0:T(8,128)S(1)}, s32[8,128]{1,0:T(8,128)S(1)}, u32[]{:S(2)}, u32[]{:S(2)}) collective-permute-start(s32[8,128]{1,0:T(8,128)S(1)} %add_add_fusion.2), channel_id=1, source_target_pairs={{0,64},{1,65},{2,66},{3,67},{4,68},{5,69},{6,70},{7,71},{8,72},{9,... | collective-permute-start | bytes 12296 | tf_op jit(solution)/shard_map/ppermute | solution.py:237
  28.1 3.9 %collective-permute-start.3 = (s32[8,128]{1,0:T(8,128)S(1)}, s32[8,128]{1,0:T(8,128)S(1)}, u32[]{:S(2)}, u32[]{:S(2)}) collective-permute-start(s32[8,128]{1,0:T(8,128)S(1)} %add_add_fusion.2), channel_id=1, source_target_pairs={{0,32},{1,33},{2,34},{3,35},{4,36},{5,37},{6,38},{7,39},{8,40},{9,... | collective-permute-start | bytes 12296 | tf_op jit(solution)/shard_map/ppermute | solution.py:237
  32.0 4.3 %collective-permute-start.6 = (s32[8,128]{1,0:T(8,128)S(1)}, s32[8,128]{1,0:T(8,128)S(1)}, u32[]{:S(2)}, u32[]{:S(2)}) collective-permute-start(s32[8,128]{1,0:T(8,128)S(1)} %add_add_fusion.1), channel_id=1, source_target_pairs={{0,128},{1,129},{2,130},{3,131},{4,132},{5,133},{6,134},{7,135},{8... | collective-permute-start | bytes 12296 | tf_op jit(solution)/shard_map/ppermute | solution.py:237
  36.3 9.7 %collective-permute-start.9 = (s32[8,128]{1,0:T(8,128)S(1)}, s32[8,128]{1,0:T(8,128)S(1)}, u32[]{:S(2)}, u32[]{:S(2)}) collective-permute-start(s32[8,128]{1,0:T(8,128)S(1)} %add.39), channel_id=1, source_target_pairs={{0,24},{1,25},{2,26},{3,27},{4,28},{5,29},{6,30},{7,31},{8,16},{9,... | collective-permute-start | bytes 12296 | tf_op jit(solution)/shard_map/ppermute | solution.py:237
  41.1 7.4 %collective-permute-start.8 = (s32[8,128]{1,0:T(8,128)S(1)}, s32[8,128]{1,0:T(8,128)S(1)}, u32[]{:S(2)}, u32[]{:S(2)}) collective-permute-start(s32[8,128]{1,0:T(8,128)S(1)} %add.39), channel_id=1, source_target_pairs={{0,16},{1,17},{2,18},{3,19},{4,20},{5,21},{6,22},{7,23},{8,24},{9,... | collective-permute-start | bytes 12296 | tf_op jit(solution)/shard_map/ppermute | solution.py:237
  42.3 6.2 %collective-permute-start.7 = (s32[8,128]{1,0:T(8,128)S(1)}, s32[8,128]{1,0:T(8,128)S(1)}, u32[]{:S(2)}, u32[]{:S(2)}) collective-permute-start(s32[8,128]{1,0:T(8,128)S(1)} %add.39), channel_id=1, source_target_pairs={{0,8},{1,9},{2,10},{3,11},{4,12},{5,13},{6,14},{7,15},{8,0},{9,1},... | collective-permute-start | bytes 12296 | tf_op jit(solution)/shard_map/ppermute | solution.py:237
  48.5 2.8 %collective-permute-start.10 = (s32[8,128]{1,0:T(8,128)S(1)}, s32[8,128]{1,0:T(8,128)S(1)}, u32[]{:S(2)}, u32[]{:S(2)}) collective-permute-start(s32[8,128]{1,0:T(8,128)S(1)} %add_add_fusion), channel_id=1, source_target_pairs={{0,4},{1,5},{2,6},{3,7},{4,0},{5,1},{6,2},{7,3},{8,12},{9,13},{10,... | collective-permute-start | bytes 12296 | tf_op jit(solution)/shard_map/ppermute | solution.py:237
  52.6 65.8 %copy-start = (bf16[1,256,4096]{2,1,0:T(8,128)(2,1)S(1)}, bf16[1,256,4096]{2,1,0:T(8,128)(2,1)}, u32[]{:S(2)}) copy-start(bf16[1,256,4096]{2,1,0:T(8,128)(2,1)} %param.8) | copy-start | bytes 6291460
  52.7 65.8 %copy-start.1 = (bf16[1,256,512]{2,1,0:T(8,128)(2,1)S(1)}, bf16[1,256,512]{2,1,0:T(8,128)(2,1)}, u32[]{:S(2)}) copy-start(bf16[1,256,512]{2,1,0:T(8,128)(2,1)} %param.9) | copy-start | bytes 786436
  52.7 65.8 %copy-start.2 = (bf16[1,256,512]{2,1,0:T(8,128)(2,1)S(1)}, bf16[1,256,512]{2,1,0:T(8,128)(2,1)}, u32[]{:S(2)}) copy-start(bf16[1,256,512]{2,1,0:T(8,128)(2,1)} %param.10) | copy-start | bytes 786436

commit v4 on v3

--- a/solution.py
+++ b/solution.py
@@ -19,7 +19,7 @@
 
 def spread_kernel(
     parent_ref, len_ref, leaf_ref, keys_ref, values_ref, out_ref, table_ref,
-    rows_scr, out_scr, in_sems, out_sems,
+    rows_scr, out_scr, table_scr, in_sems, out_sems, table_sem,
 ):
     _, tok, width = rows_scr.shape
     blocks, heads = tok // BLK, width // HEAD_DIM // 2
@@ -34,7 +34,17 @@
     for load in loads:
         load.start()
 
-    stores = []
+    me = lax.axis_index("req") * lax.axis_size("head") + lax.axis_index("head")
+    nodes = table_scr.shape[0] * table_scr.shape[1] // 4
+    spot = lax.broadcasted_iota(jnp.int32, table_scr.shape, 0) * table_scr.shape[1]
+    spot = spot + lax.broadcasted_iota(jnp.int32, table_scr.shape, 1) - me
+    table = jnp.zeros(table_scr.shape, jnp.int32)
+    for i, ref in enumerate((parent_ref, len_ref, leaf_ref)):
+        table = jnp.where(spot == i * nodes, ref[0], table)
+    table_scr[...] = table
+    stores = [pltpu.make_async_copy(table_scr, table_ref, table_sem)]
+    stores[0].start()
+
     for kv in range(2):
         for c in range(CUTS):
             loads[kv * CUTS + c].wait()
@@ -53,15 +63,6 @@
                 )
             )
             stores[-1].start()
-    me = lax.axis_index("req") * lax.axis_size("head") + lax.axis_index("head")
-    nodes = table_ref.shape[0] * table_ref.shape[1] // 4
-    spot = lax.broadcasted_iota(jnp.int32, table_ref.shape, 0) * table_ref.shape[1]
-    spot = spot + lax.broadcasted_iota(jnp.int32, table_ref.shape, 1) - me
-    table = jnp.zeros(table_ref.shape, jnp.int32)
-    for i, ref in enumerate((parent_ref, len_ref, leaf_ref)):
-        table = jnp.where(spot == i * nodes, ref[...], table)
-    table_ref[...] = table
-
     for store in stores:
         store.wait()
 
@@ -76,49 +77,44 @@
             jax.ShapeDtypeStruct((pieces, BLK, HEAD_DIM), keys.dtype),
             jax.ShapeDtypeStruct((4 * count // 128, 128), jnp.int32),
         ),
-        in_specs=[pl.BlockSpec(memory_space=pltpu.VMEM)] * 3
+        in_specs=[pl.BlockSpec(memory_space=pltpu.SMEM)] * 3
         + [pl.BlockSpec(memory_space=pl.ANY)] * 2,
-        out_specs=(
-            pl.BlockSpec(memory_space=pl.ANY),
-            pl.BlockSpec(memory_space=pltpu.VMEM),
-        ),
+        out_specs=(pl.BlockSpec(memory_space=pl.ANY),) * 2,
         scratch_shapes=[
             pltpu.VMEM((2, tok, width), keys.dtype),
             pltpu.VMEM((pieces, BLK, HEAD_DIM), keys.dtype),
+            pltpu.VMEM((4 * count // 128, 128), jnp.int32),
             pltpu.SemaphoreType.DMA((2 * CUTS,)),
             pltpu.SemaphoreType.DMA((2 * heads,)),
+            pltpu.SemaphoreType.DMA,
         ],
         compiler_params=pltpu.CompilerParams(vmem_limit_bytes=60 << 20),
-    )(*(x.reshape(1, 1) for x in (parents, node_len, req_leaf)), keys, values)
-
-
-def pick_kernel(reqs_step, table_ref, pieces_ref, out_ref):
+    )(parents, node_len, req_leaf, keys, values)
+
+
+def pick_kernel(table_ref, pieces_ref, out_ref):
     nodes = pieces_ref.shape[0]
-    base = pl.program_id(0) * reqs_step
 
     def one(r, carry):
-        node = table_ref[2 * nodes + 2 * (base + r)]
+        node = table_ref[2 * nodes + 2 * r]
         for i in range(DEPTH):
             out_ref[r, i * BLK:(i + 1) * BLK, :] = pieces_ref[node]
             if i < DEPTH - 1:
                 node = table_ref[node]
         return carry
 
-    lax.fori_loop(0, reqs_step, one, 0, unroll=8)
+    lax.fori_loop(0, out_ref.shape[0], one, 0, unroll=8)
 
 
 def pick(table, pieces, reqs):
-    steps = 4
-    reqs_step = reqs // steps
     return pl.pallas_call(
-        functools.partial(pick_kernel, reqs_step),
+        pick_kernel,
         out_shape=jax.ShapeDtypeStruct((reqs, DEPTH * BLK, HEAD_DIM), pieces.dtype),
-        grid_spec=pltpu.PrefetchScalarGridSpec(
-            num_scalar_prefetch=1,
-            grid=(steps,),
-            in_specs=[pl.BlockSpec(pieces.shape, lambda s, t: (0, 0, 0))],
-            out_specs=pl.BlockSpec((reqs_step, DEPTH * BLK, HEAD_DIM), lambda s, t: (s, 0, 0)),
-        ),
+        in_specs=[
+            pl.BlockSpec(memory_space=pltpu.SMEM),
+            pl.BlockSpec(memory_space=pltpu.VMEM),
+        ],
+        out_specs=pl.BlockSpec(memory_space=pltpu.VMEM),
         compiler_params=pltpu.CompilerParams(vmem_limit_bytes=32 << 20),
     )(table, pieces)
 

time: 133 us -> 132 us (level)
  no operation moved by 1% of the time
where the time goes in v4:
time: 132 us
  blocking collectives  65.8 us (50%)
  starting transfers between devices  32.6 us (25%)
  Pallas kernels  17.1 us (13%)
  waiting for transfers between devices  13.9 us (11%)
  between operations  2.19 us (2%)
    all_to_all x1, blocking collectives, per_device(): lax.all_to_all(picked, 'req', split_axis=0, concat_axis=0, tiled=True)  65.8 us
    ppermute x11, starting transfers between devices, share_ints(): lax.ppermute(table, ('req', 'head'), [(i, i ^ flip) for i in range(count)])  17 us
    all_to_all x1, starting transfers between devices, per_device(): lax.all_to_all(sent, ('req', 'head'), split_axis=0, concat_axis=0, tiled=...  15.7 us
    ppermute x11, waiting for transfers between devices, share_ints(): lax.ppermute(table, ('req', 'head'), [(i, i ^ flip) for i in range(count)])  13.8 us
    pallas_call x1, Pallas kernels, attend(): pl.pallas_call(attend_kernel, out_shape=jax.ShapeDtypeStruct((suf, width)...  13.7 us
  transfers between devices with their start and end apart: 12, of which 7 were waited for; matrix products, arithmetic and copies ran while one was open for 0% of the time, Pallas kernels for 0%

profile of v4, /device:TPU:1, one launch (start us, length us, event | category | flops | bytes accessed | tf_op | source)
XLA Modules:
  0.0 131.6 jit_solution(5205103771292266421)
XLA Ops:
  1.9 2.2 %shard_map.82 = (bf16[256,16,128]{2,1,0:T(8,128)(2,1)}, s32[8,128]{1,0:T(8,128)}) custom-call(s32[1]{0:T(128)S(6)} %copy.9.parent_ref, s32[1]{0:T(128)S(6)} %copy.10.len_ref, s32[1]{0:T(128)S(6)} %copy.11.leaf_ref, bf16[256,1024]{1,0:T(8,128)(2,1)} %bitcast.11, bf16[256,1024]{1,0:T(8,128)(2,1)} %bitcast.12), custom_call_target="tpu_custom_call" | custom-call | tf_op jit(solution)/shard_map/pallas_call | solution.py:74
  4.2 0.0 copy-start.3
  4.2 15.7 %all-to-all-start = ((bf16[256,16,128]{2,1,0:T(8,128)(2,1)}), bf16[256,16,128]{2,1,0:T(8,128)(2,1)S(1)}, u32[]{:S(2)}, u32[]{:S(2)}) async-start(bf16[256,16,128]{2,1,0:T(8,128)(2,1)} %get-tuple-element.8), calls=%async_computation | async-start | bytes 2097152 | tf_op jit(solution)/shard_map/all_to_all | solution.py:247
  19.9 0.0 copy-done.3
  19.9 1.7 %collective-permute-start.2 = (s32[8,128]{1,0:T(8,128)S(1)}, s32[8,128]{1,0:T(8,128)S(1)}, u32[]{:S(2)}, u32[]{:S(2)}) collective-permute-start(s32[8,128]{1,0:T(8,128)S(1)} %copy-done.3), channel_id=1, source_target_pairs={{0,3},{1,2},{2,1},{3,0},{4,7},{5,6},{6,5},{7,4},{8,11},{9,10},{10,... | collective-permute-start | bytes 12296 | tf_op jit(solution)/shard_map/ppermute | solution.py:233
  21.6 0.6 collective-permute-start.1
  22.2 1.3 collective-permute-start
  23.5 0.0 collective-permute-done.2
  23.5 0.0 collective-permute-done.1
  23.5 1.8 %collective-permute-done = s32[8,128]{1,0:T(8,128)S(1)} collective-permute-done((s32[8,128]{1,0:T(8,128)S(1)}, s32[8,128]{1,0:T(8,128)S(1)}, u32[]{:S(2)}, u32[]{:S(2)}) %collective-permute-start) | collective-permute-done | bytes 4128 | tf_op jit(solution)/shard_map/ppermute | solution.py:233
  25.3 1.8 %collective-permute-start.5 = (s32[8,128]{1,0:T(8,128)S(1)}, s32[8,128]{1,0:T(8,128)S(1)}, u32[]{:S(2)}, u32[]{:S(2)}) collective-permute-start(s32[8,128]{1,0:T(8,128)S(1)} %add_add_fusion.2), channel_id=1, source_target_pairs={{0,96},{1,97},{2,98},{3,99},{4,100},{5,101},{6,102},{7,103},{8,104... | collective-permute-start | bytes 12296 | tf_op jit(solution)/shard_map/ppermute | solution.py:233
  27.1 0.4 collective-permute-start.4
  27.5 1.0 collective-permute-start.3
  28.5 0.7 collective-permute-done.5
  29.3 2.1 %collective-permute-done.4 = s32[8,128]{1,0:T(8,128)S(1)} collective-permute-done((s32[8,128]{1,0:T(8,128)S(1)}, s32[8,128]{1,0:T(8,128)S(1)}, u32[]{:S(2)}, u32[]{:S(2)}) %collective-permute-start.4) | collective-permute-done | bytes 4128 | tf_op jit(solution)/shard_map/ppermute | solution.py:233
  31.4 0.0 collective-permute-done.3
  31.4 2.6 %collective-permute-start.6 = (s32[8,128]{1,0:T(8,128)S(1)}, s32[8,128]{1,0:T(8,128)S(1)}, u32[]{:S(2)}, u32[]{:S(2)}) collective-permute-start(s32[8,128]{1,0:T(8,128)S(1)} %add_add_fusion.1), channel_id=1, source_target_pairs={{0,128},{1,129},{2,130},{3,131},{4,132},{5,133},{6,134},{7,135},{8... | collective-permute-start | bytes 12296 | tf_op jit(solution)/shard_map/ppermute | solution.py:233
  34.0 1.8 %collective-permute-done.6 = s32[8,128]{1,0:T(8,128)S(1)} collective-permute-done((s32[8,128]{1,0:T(8,128)S(1)}, s32[8,128]{1,0:T(8,128)S(1)}, u32[]{:S(2)}, u32[]{:S(2)}) %collective-permute-start.6) | collective-permute-done | bytes 4128 | tf_op jit(solution)/shard_map/ppermute | solution.py:233
  35.8 4.8 %collective-permute-start.9 = (s32[8,128]{1,0:T(8,128)S(1)}, s32[8,128]{1,0:T(8,128)S(1)}, u32[]{:S(2)}, u32[]{:S(2)}) collective-permute-start(s32[8,128]{1,0:T(8,128)S(1)} %add.39), channel_id=1, source_target_pairs={{0,24},{1,25},{2,26},{3,27},{4,28},{5,29},{6,30},{7,31},{8,16},{9,... | collective-permute-start | bytes 12296 | tf_op jit(solution)/shard_map/ppermute | solution.py:233
  40.5 1.2 collective-permute-start.8
  41.7 0.9 collective-permute-start.7
  42.6 2.9 %collective-permute-done.9 = s32[8,128]{1,0:T(8,128)S(1)} collective-permute-done((s32[8,128]{1,0:T(8,128)S(1)}, s32[8,128]{1,0:T(8,128)S(1)}, u32[]{:S(2)}, u32[]{:S(2)}) %collective-permute-start.9) | collective-permute-done | bytes 4128 | tf_op jit(solution)/shard_map/ppermute | solution.py:233
  45.5 2.4 %collective-permute-done.8 = s32[8,128]{1,0:T(8,128)S(1)} collective-permute-done((s32[8,128]{1,0:T(8,128)S(1)}, s32[8,128]{1,0:T(8,128)S(1)}, u32[]{:S(2)}, u32[]{:S(2)}) %collective-permute-start.8) | collective-permute-done | bytes 4128 | tf_op jit(solution)/shard_map/ppermute | solution.py:233
  47.9 0.0 collective-permute-done.7
  47.9 0.7 collective-permute-start.10
  48.6 2.2 %collective-permute-done.10 = s32[8,128]{1,0:T(8,128)S(1)} collective-permute-done((s32[8,128]{1,0:T(8,128)S(1)}, s32[8,128]{1,0:T(8,128)S(1)}, u32[]{:S(2)}, u32[]{:S(2)}) %collective-permute-start.10) | collective-permute-done | bytes 4128 | tf_op jit(solution)/shard_map/ppermute | solution.py:233
  50.7 0.0 all-to-all-done.pieces_ref
  50.7 1.2 shard_map.83
  51.9 0.0 copy-start
  51.9 0.0 copy-start.1
  51.9 0.0 copy-start.2
  51.9 65.8 %all_to_all.10.prefix_ref = bf16[128,64,128]{2,1,0:T(8,128)(2,1)S(1)} all-to-all(bf16[128,64,128]{2,1,0:T(8,128)(2,1)S(1)} %shard_map.83), channel_id=1, replica_groups=mesh['req'=128,'head'=2] {'req'}, dimensions={0} | all-to-all | bytes 4194304 | tf_op jit(solution)/shard_map/all_to_all | solution.py:250
  117.7 0.0 copy-done
  117.7 0.0 copy-done.1
  117.7 0.0 copy-done.2
  117.8 13.7 %shard_map.84 = bf16[256,4096]{1,0:T(8,128)(2,1)} custom-call(s32[1024]{0:T(1024)S(1)} %add_bitcast_fusion.table_ref, bf16[256,4096]{1,0:T(8,128)(2,1)S(1)} %bitcast.8, bf16[256,512]{1,0:T(8,128)(2,1)S(1)} %bitcast.9, bf16[256,512]{1,0:T(8,128)(2,1)S(1)} %bitcast.10, bf16[128,64,128]{2,1,0:T(8,128)(2,1)S(1)} %all_to_all.10.prefix_ref), custom_call_target="tpu_custom_call" | custom-call | tf_op jit(solution)/shard_map/pallas_call | solution.py:210
  (5 shorter events, 0.0 us)
Async XLA Ops:
  4.2 15.7 %copy-start.3 = (s32[8,128]{1,0:T(8,128)S(1)}, s32[8,128]{1,0:T(8,128)}, u32[]{:S(2)}) copy-start(s32[8,128]{1,0:T(8,128)} %get-tuple-element.7) | copy-start | bytes 12292
  4.2 46.5 %all-to-all-start = ((bf16[256,16,128]{2,1,0:T(8,128)(2,1)}), bf16[256,16,128]{2,1,0:T(8,128)(2,1)S(1)}, u32[]{:S(2)}, u32[]{:S(2)}) async-start(bf16[256,16,128]{2,1,0:T(8,128)(2,1)} %get-tuple-element.8), calls=%async_computation | async-start | bytes 2097152 | tf_op jit(solution)/shard_map/all_to_all | solution.py:247
  19.9 3.6 %collective-permute-start.2 = (s32[8,128]{1,0:T(8,128)S(1)}, s32[8,128]{1,0:T(8,128)S(1)}, u32[]{:S(2)}, u32[]{:S(2)}) collective-permute-start(s32[8,128]{1,0:T(8,128)S(1)} %copy-done.3), channel_id=1, source_target_pairs={{0,3},{1,2},{2,1},{3,0},{4,7},{5,6},{6,5},{7,4},{8,11},{9,10},{10,... | collective-permute-start | bytes 12296 | tf_op jit(solution)/shard_map/ppermute | solution.py:233
  21.6 1.9 %collective-permute-start.1 = (s32[8,128]{1,0:T(8,128)S(1)}, s32[8,128]{1,0:T(8,128)S(1)}, u32[]{:S(2)}, u32[]{:S(2)}) collective-permute-start(s32[8,128]{1,0:T(8,128)S(1)} %copy-done.3), channel_id=1, source_target_pairs={{0,2},{1,3},{2,0},{3,1},{4,6},{5,7},{6,4},{7,5},{8,10},{9,11},{10,... | collective-permute-start | bytes 12296 | tf_op jit(solution)/shard_map/ppermute | solution.py:233
  22.2 3.1 %collective-permute-start = (s32[8,128]{1,0:T(8,128)S(1)}, s32[8,128]{1,0:T(8,128)S(1)}, u32[]{:S(2)}, u32[]{:S(2)}) collective-permute-start(s32[8,128]{1,0:T(8,128)S(1)} %copy-done.3), channel_id=1, source_target_pairs={{0,1},{1,0},{2,3},{3,2},{4,5},{5,4},{6,7},{7,6},{8,9},{9,8},{10,11... | collective-permute-start | bytes 12296 | tf_op jit(solution)/shard_map/ppermute | solution.py:233
  25.3 4.0 %collective-permute-start.5 = (s32[8,128]{1,0:T(8,128)S(1)}, s32[8,128]{1,0:T(8,128)S(1)}, u32[]{:S(2)}, u32[]{:S(2)}) collective-permute-start(s32[8,128]{1,0:T(8,128)S(1)} %add_add_fusion.2), channel_id=1, source_target_pairs={{0,96},{1,97},{2,98},{3,99},{4,100},{5,101},{6,102},{7,103},{8,104... | collective-permute-start | bytes 12296 | tf_op jit(solution)/shard_map/ppermute | solution.py:233
  27.1 4.3 %collective-permute-start.4 = (s32[8,128]{1,0:T(8,128)S(1)}, s32[8,128]{1,0:T(8,128)S(1)}, u32[]{:S(2)}, u32[]{:S(2)}) collective-permute-start(s32[8,128]{1,0:T(8,128)S(1)} %add_add_fusion.2), channel_id=1, source_target_pairs={{0,64},{1,65},{2,66},{3,67},{4,68},{5,69},{6,70},{7,71},{8,72},{9,... | collective-permute-start | bytes 12296 | tf_op jit(solution)/shard_map/ppermute | solution.py:233
  27.5 3.9 %collective-permute-start.3 = (s32[8,128]{1,0:T(8,128)S(1)}, s32[8,128]{1,0:T(8,128)S(1)}, u32[]{:S(2)}, u32[]{:S(2)}) collective-permute-start(s32[8,128]{1,0:T(8,128)S(1)} %add_add_fusion.2), channel_id=1, source_target_pairs={{0,32},{1,33},{2,34},{3,35},{4,36},{5,37},{6,38},{7,39},{8,40},{9,... | collective-permute-start | bytes 12296 | tf_op jit(solution)/shard_map/ppermute | solution.py:233
  31.4 4.3 %collective-permute-start.6 = (s32[8,128]{1,0:T(8,128)S(1)}, s32[8,128]{1,0:T(8,128)S(1)}, u32[]{:S(2)}, u32[]{:S(2)}) collective-permute-start(s32[8,128]{1,0:T(8,128)S(1)} %add_add_fusion.1), channel_id=1, source_target_pairs={{0,128},{1,129},{2,130},{3,131},{4,132},{5,133},{6,134},{7,135},{8... | collective-permute-start | bytes 12296 | tf_op jit(solution)/shard_map/ppermute | solution.py:233
  35.8 9.7 %collective-permute-start.9 = (s32[8,128]{1,0:T(8,128)S(1)}, s32[8,128]{1,0:T(8,128)S(1)}, u32[]{:S(2)}, u32[]{:S(2)}) collective-permute-start(s32[8,128]{1,0:T(8,128)S(1)} %add.39), channel_id=1, source_target_pairs={{0,24},{1,25},{2,26},{3,27},{4,28},{5,29},{6,30},{7,31},{8,16},{9,... | collective-permute-start | bytes 12296 | tf_op jit(solution)/shard_map/ppermute | solution.py:233
  40.5 7.4 %collective-permute-start.8 = (s32[8,128]{1,0:T(8,128)S(1)}, s32[8,128]{1,0:T(8,128)S(1)}, u32[]{:S(2)}, u32[]{:S(2)}) collective-permute-start(s32[8,128]{1,0:T(8,128)S(1)} %add.39), channel_id=1, source_target_pairs={{0,16},{1,17},{2,18},{3,19},{4,20},{5,21},{6,22},{7,23},{8,24},{9,... | collective-permute-start | bytes 12296 | tf_op jit(solution)/shard_map/ppermute | solution.py:233
  41.7 6.2 %collective-permute-start.7 = (s32[8,128]{1,0:T(8,128)S(1)}, s32[8,128]{1,0:T(8,128)S(1)}, u32[]{:S(2)}, u32[]{:S(2)}) collective-permute-start(s32[8,128]{1,0:T(8,128)S(1)} %add.39), channel_id=1, source_target_pairs={{0,8},{1,9},{2,10},{3,11},{4,12},{5,13},{6,14},{7,15},{8,0},{9,1},... | collective-permute-start | bytes 12296 | tf_op jit(solution)/shard_map/ppermute | solution.py:233
  47.9 2.8 %collective-permute-start.10 = (s32[8,128]{1,0:T(8,128)S(1)}, s32[8,128]{1,0:T(8,128)S(1)}, u32[]{:S(2)}, u32[]{:S(2)}) collective-permute-start(s32[8,128]{1,0:T(8,128)S(1)} %add_add_fusion), channel_id=1, source_target_pairs={{0,4},{1,5},{2,6},{3,7},{4,0},{5,1},{6,2},{7,3},{8,12},{9,13},{10,... | collective-permute-start | bytes 12296 | tf_op jit(solution)/shard_map/ppermute | solution.py:233
  51.9 65.8 %copy-start = (bf16[1,256,4096]{2,1,0:T(8,128)(2,1)S(1)}, bf16[1,256,4096]{2,1,0:T(8,128)(2,1)}, u32[]{:S(2)}) copy-start(bf16[1,256,4096]{2,1,0:T(8,128)(2,1)} %param.8) | copy-start | bytes 6291460
  51.9 65.8 %copy-start.1 = (bf16[1,256,512]{2,1,0:T(8,128)(2,1)S(1)}, bf16[1,256,512]{2,1,0:T(8,128)(2,1)}, u32[]{:S(2)}) copy-start(bf16[1,256,512]{2,1,0:T(8,128)(2,1)} %param.9) | copy-start | bytes 786436
  51.9 65.8 %copy-start.2 = (bf16[1,256,512]{2,1,0:T(8,128)(2,1)S(1)}, bf16[1,256,512]{2,1,0:T(8,128)(2,1)}, u32[]{:S(2)}) copy-start(bf16[1,256,512]{2,1,0:T(8,128)(2,1)} %param.10) | copy-start | bytes 786436
